TPU v7x, 256 devices: a whole 4x4x8 slice. The times are simulated.
256 devices in a mesh: slab: 64 (over x, z, y_hi), head: 4 (over y_lo, core).
Axes of the slice: x: 4, y: 4 (y_hi: 2, y_lo: 2; y = y_hi * 2 + y_lo), z: 8, core: 2. Of those that a mesh axis runs over, the one named last changes fastest.
Arguments:
- queries: bfloat16 [24576, 3072], P(('slab', 'head')), may hold values from -200 to 200
- keys: bfloat16 [24576, 3072], P(('slab', 'head')), may hold values from -6 to 6
- values: bfloat16 [24576, 3072], P(('slab', 'head')), may hold values from -48 to 48
- windows: int32 [24, 3], replicated, may hold values from 0 to 1
Outputs:
- attended: bfloat16 [24576, 3072], P(('slab', 'head'))
All inputs are finite; a program needn't handle non-finite values.
Results may differ from a plain program's by a relative error of at most 0.0049.
Values may be sent and summed in bfloat16 or wider, within the bound.
A program may use at most 128 MiB of HBM per device.

v0:
```python
import jax
import jax.numpy as jnp
from jax import lax
from jax.sharding import PartitionSpec as P

HTILES = 4


neg_fill = -1e30


def from_partner(block, axis, distance):
    count = lax.axis_size(axis)
    route = []
    for low in range(count):
        high = low | 1 << distance
        if high != low and high < count:
            route += [(low, high), (high, low)]
    return lax.ppermute(block, axis, route)


def from_behind(value, axis, by):
    devices = lax.axis_size(axis)
    pairs = [(i, i + by) for i in range(devices) if 0 <= i + by < devices]
    return lax.ppermute(value, axis, pairs)


def attend(query, keys_flat, vals_flat, keep, scale):
    scores = jnp.einsum("qd,kd->qk", query, keys_flat, preferred_element_type=jnp.float32) * scale
    scores = jnp.where(keep[None, :], scores, neg_fill)
    top = jnp.max(scores, axis=1, keepdims=True)
    expo = jnp.exp(scores - top)
    weights = (expo / jnp.sum(expo, axis=1, keepdims=True)).astype(jnp.bfloat16)
    return jnp.dot(weights, vals_flat, preferred_element_type=jnp.float32).astype(jnp.bfloat16)


def shards(queries, keys, values, windows):
    groups = lax.axis_size("head")
    tok_local, width = queries.shape
    heads_all = windows.shape[0]
    head_dim = width // heads_all
    heads_local = heads_all // groups
    local_width = heads_local * head_dim
    tile = tok_local * groups
    slabs = lax.axis_size("slab")
    wtiles = slabs // 8
    partner_bit = (slabs // 2).bit_length() - 1
    scale = head_dim ** (-0.5)
    q_tile, k_tile, v_tile = (
        lax.all_to_all(queries, "head", split_axis=1, concat_axis=0, tiled=True),
        lax.all_to_all(keys, "head", split_axis=1, concat_axis=0, tiled=True),
        lax.all_to_all(values, "head", split_axis=1, concat_axis=0, tiled=True),
    )
    paired = jnp.stack([k_tile, v_tile])
    other = from_partner(paired, "slab", partner_bit)
    both = jnp.stack([paired, other])
    grid_rows = []
    for step_h in (-1, 0, 1):
        row_tiles = []
        for step_w in (-1, 0, 1):
            if step_h == 0 and step_w == 0:
                row_tiles.append(both)
            else:
                row_tiles.append(from_behind(both, "slab", -(step_h * wtiles + step_w)))
        grid_rows.append(jnp.stack(row_tiles, axis=1))
    key_grid = jnp.stack(grid_rows, axis=1)
    slab_index = lax.axis_index("slab")
    h_pos = slab_index // wtiles % HTILES
    w_pos = slab_index % wtiles
    offsets = jnp.arange(3, dtype=jnp.int32) - 1
    distance = jnp.abs(offsets)
    h_valid = (h_pos + offsets >= 0) & (h_pos + offsets < HTILES)
    w_valid = (w_pos + offsets >= 0) & (w_pos + offsets < wtiles)
    time_index = jnp.arange(2, dtype=jnp.int32)
    reach = lax.dynamic_slice_in_dim(windows, lax.axis_index("head") * heads_local, heads_local, 0)

    def one_head(index, result):
        column_start = index * head_dim
        query_head = lax.dynamic_slice_in_dim(q_tile, column_start, head_dim, 1)
        near_head = lax.dynamic_slice_in_dim(key_grid, column_start, head_dim, 5)
        reach_t = reach[index, 0]
        h_keep = h_valid & (distance <= reach[index, 1])
        w_keep = w_valid & (distance <= reach[index, 2])
        plane = (h_keep[:, None] & w_keep[None, :]).reshape(9)
        time_keep = time_index <= reach_t
        allowed = (time_keep[:, None] & plane[None, :]).reshape(18)
        keep = jnp.repeat(allowed, tile, total_repeat_length=18 * tile)
        keys_flat = near_head[:, :, :, 0].reshape(18 * tile, head_dim)
        vals_flat = near_head[:, :, :, 1].reshape(18 * tile, head_dim)
        piece = attend(query_head, keys_flat, vals_flat, keep, scale)
        return lax.dynamic_update_slice_in_dim(result, piece, column_start, 1)

    result = lax.fori_loop(0, heads_local, one_head, jnp.zeros((tile, local_width), jnp.bfloat16))
    return lax.all_to_all(result, "head", split_axis=0, concat_axis=1, tiled=True)


def solution(mesh):
    return jax.shard_map(
        shards,
        mesh=mesh,
        in_specs=(
            P(("slab", "head"), None),
            P(("slab", "head"), None),
            P(("slab", "head"), None),
            P(),
        ),
        out_specs=P(("slab", "head"), None),
        check_vma=False,
    )
```

profile of v0, /device:TPU:162, one launch (start us, length us, event | category | flops | bytes accessed | tf_op | source)
XLA Modules:
  0.0 1002.3 jit_solution(4332496897229386795)
XLA Ops:
  1.9 3.6 all-to-all-start.1
  6.7 8.4 all-to-all-done.1
  15.1 11.9 %all_to_all.70 = bf16[96,4,768]{2,0,1:T(8,128)(2,1)S(1)} all-to-all(bf16[96,4,768]{2,0,1:T(8,128)(2,1)S(1)} %bitcast.130), channel_id=1, replica_groups=mesh['slab'=64,'head'=4] {'head'}, dimensions={1} | all-to-all | bytes 1179648 | tf_op jit(solution)/shard_map/all_to_all | solution.py:52
  29.4 27.0 %collective-permute-done = bf16[2,384,768]{2,1,0:T(8,128)(2,1)S(1)} collective-permute-done((bf16[2,384,768]{2,1,0:T(8,128)(2,1)S(1)}, bf16[2,384,768]{2,1,0:T(8,128)(2,1)S(1)}, u32[]{:S(2)}, u32[]{:S(2)}) %collective-permute-start) | collective-permute-done | bytes 1179680 | tf_op jit(solution)/shard_map/ppermute | solution.py:19
  58.1 4.2 collective-permute-start.6
  62.3 8.2 collective-permute-start.7
  72.4 4.9 collective-permute-start.4
  77.3 3.4 collective-permute-start.5
  80.6 208.2 %collective-permute-done.6 = bf16[2,2,384,768]{3,2,1,0:T(8,128)(2,1)} collective-permute-done((bf16[2,2,384,768]{3,2,1,0:T(8,128)(2,1)}, bf16[2,2,384,768]{3,2,1,0:T(8,128)(2,1)}, u32[]{:S(2)}, u32[]{:S(2)}) %collective-permute-start.6) | collective-permute-done | bytes 2359328 | tf_op jit(solution)/shard_map/ppermute | solution.py:25
  290.8 138.4 %collective-permute-start.1 = (bf16[2,2,384,768]{3,2,1,0:T(8,128)(2,1)}, bf16[2,2,384,768]{3,2,1,0:T(8,128)(2,1)}, u32[]{:S(2)}, u32[]{:S(2)}) collective-permute-start(bf16[2,2,384,768]{3,2,1,0:T(8,128)(2,1)} %get-tuple-element.473), channel_id=1, source_target_pairs={{0,36},{4,40},{8,44},{12,48},{16,52},{20,56},{24,60},{28,64},{32,6... | collective-permute-start | bytes 7077896 | tf_op jit(solution)/shard_map/ppermute | solution.py:25
  429.2 70.1 %collective-permute-done.8 = bf16[2,2,384,768]{3,2,1,0:T(8,128)(2,1)} collective-permute-done((bf16[2,2,384,768]{3,2,1,0:T(8,128)(2,1)}, bf16[2,2,384,768]{3,2,1,0:T(8,128)(2,1)}, u32[]{:S(2)}, u32[]{:S(2)}) %collective-permute-start.8) | collective-permute-done | bytes 2359328 | tf_op jit(solution)/shard_map/ppermute | solution.py:25
  502.1 22.1 %all-to-all-start = ((bf16[96,4,768]{2,0,1:T(8,128)(2,1)}), bf16[96,4,768]{2,0,1:T(8,128)(2,1)S(1)}, u32[]{:S(2)}, u32[]{:S(2)}) async-start(bf16[96,4,768]{2,0,1:T(8,128)(2,1)} %bitcast.74), calls=%async_computation | async-start | bytes 1179648 | tf_op jit(solution)/shard_map/all_to_all | solution.py:50
  524.3 3.9 maximum_bitcast_fusion.2
  531.5 245.5 %collective-permute-done.3 = bf16[2,2,384,768]{3,2,1,0:T(8,128)(2,1)} collective-permute-done((bf16[2,2,384,768]{3,2,1,0:T(8,128)(2,1)}, bf16[2,2,384,768]{3,2,1,0:T(8,128)(2,1)}, u32[]{:S(2)}, u32[]{:S(2)}) %collective-permute-start.3) | collective-permute-done | bytes 2359328 | tf_op jit(solution)/shard_map/ppermute | solution.py:25
  777.0 23.1 %collective-permute-done.1 = bf16[2,2,384,768]{3,2,1,0:T(8,128)(2,1)} collective-permute-done((bf16[2,2,384,768]{3,2,1,0:T(8,128)(2,1)}, bf16[2,2,384,768]{3,2,1,0:T(8,128)(2,1)}, u32[]{:S(2)}, u32[]{:S(2)}) %collective-permute-start.1) | collective-permute-done | bytes 2359328 | tf_op jit(solution)/shard_map/ppermute | solution.py:25
  800.3 9.8 pad_maximum_fusion
  810.4 139.9 %while.22 = (s32[]{:T(128)}, bf16[384,768]{1,0:T(8,128)(2,1)S(1)}, s32[6,3]{0,1:T(4,128)S(1)}, bf16[384,768]{1,0:T(8,128)(2,1)S(1)}, bf16[2,3,3,2,384,768]{5,4,3...) while((s32[]{:T(128)}, bf16[384,768]{1,0:T(8,128)(2,1)S(1)}, ...), condition=%wide.region_3.4_spmd.clone.clone, body=%wide.region_0.3_spmd.clone.clone.sunk | while | flops 1380354048 | bytes 42804760 | solution.py:93
  814.0 11.3 %select_select_fusion.2 = pred[6912]{0:T(1024)(128)(4,1)S(1)} fusion(pred[6912]{0:T(1024)(128)(4,1)S(1)} %get-tuple-element.643, pred[6912]{0:T(1024)(128)(4,1)S(1)} %get-tuple-element.644, pred[6912]{0:T(1024)(128)(4,1)S(1)} %get-tuple-element.645, pred[6912]{0:T(1024)(128)(4,1)S(1)} %get-tuple-element.646, ...), kind=kLoop, calls=%fused_computation.12.clone.1 | loop fusion | flops 117504 | bytes 124434 | tf_op jit(solution)/shard_map/while/body/eval_jaxpr/jit(_take)/gather | solution.py:87
  837.4 11.3 %select_select_fusion.2 = pred[6912]{0:T(1024)(128)(4,1)S(1)} fusion(pred[6912]{0:T(1024)(128)(4,1)S(1)} %get-tuple-element.643, pred[6912]{0:T(1024)(128)(4,1)S(1)} %get-tuple-element.644, pred[6912]{0:T(1024)(128)(4,1)S(1)} %get-tuple-element.645, pred[6912]{0:T(1024)(128)(4,1)S(1)} %get-tuple-element.646, ...), kind=kLoop, calls=%fused_computation.12.clone.1 | loop fusion | flops 117504 | bytes 124434 | tf_op jit(solution)/shard_map/while/body/eval_jaxpr/jit(_take)/gather | solution.py:87
  860.7 11.3 %select_select_fusion.2 = pred[6912]{0:T(1024)(128)(4,1)S(1)} fusion(pred[6912]{0:T(1024)(128)(4,1)S(1)} %get-tuple-element.643, pred[6912]{0:T(1024)(128)(4,1)S(1)} %get-tuple-element.644, pred[6912]{0:T(1024)(128)(4,1)S(1)} %get-tuple-element.645, pred[6912]{0:T(1024)(128)(4,1)S(1)} %get-tuple-element.646, ...), kind=kLoop, calls=%fused_computation.12.clone.1 | loop fusion | flops 117504 | bytes 124434 | tf_op jit(solution)/shard_map/while/body/eval_jaxpr/jit(_take)/gather | solution.py:87
  884.0 11.3 %select_select_fusion.2 = pred[6912]{0:T(1024)(128)(4,1)S(1)} fusion(pred[6912]{0:T(1024)(128)(4,1)S(1)} %get-tuple-element.643, pred[6912]{0:T(1024)(128)(4,1)S(1)} %get-tuple-element.644, pred[6912]{0:T(1024)(128)(4,1)S(1)} %get-tuple-element.645, pred[6912]{0:T(1024)(128)(4,1)S(1)} %get-tuple-element.646, ...), kind=kLoop, calls=%fused_computation.12.clone.1 | loop fusion | flops 117504 | bytes 124434 | tf_op jit(solution)/shard_map/while/body/eval_jaxpr/jit(_take)/gather | solution.py:87
  907.3 11.3 %select_select_fusion.2 = pred[6912]{0:T(1024)(128)(4,1)S(1)} fusion(pred[6912]{0:T(1024)(128)(4,1)S(1)} %get-tuple-element.643, pred[6912]{0:T(1024)(128)(4,1)S(1)} %get-tuple-element.644, pred[6912]{0:T(1024)(128)(4,1)S(1)} %get-tuple-element.645, pred[6912]{0:T(1024)(128)(4,1)S(1)} %get-tuple-element.646, ...), kind=kLoop, calls=%fused_computation.12.clone.1 | loop fusion | flops 117504 | bytes 124434 | tf_op jit(solution)/shard_map/while/body/eval_jaxpr/jit(_take)/gather | solution.py:87
  930.7 11.3 %select_select_fusion.2 = pred[6912]{0:T(1024)(128)(4,1)S(1)} fusion(pred[6912]{0:T(1024)(128)(4,1)S(1)} %get-tuple-element.643, pred[6912]{0:T(1024)(128)(4,1)S(1)} %get-tuple-element.644, pred[6912]{0:T(1024)(128)(4,1)S(1)} %get-tuple-element.645, pred[6912]{0:T(1024)(128)(4,1)S(1)} %get-tuple-element.646, ...), kind=kLoop, calls=%fused_computation.12.clone.1 | loop fusion | flops 117504 | bytes 124434 | tf_op jit(solution)/shard_map/while/body/eval_jaxpr/jit(_take)/gather | solution.py:87
  950.4 51.0 %all_to_all.71 = bf16[4,96,768]{2,1,0:T(8,128)(2,1)S(1)} all-to-all(bf16[4,96,768]{2,1,0:T(8,128)(2,1)S(1)} %bitcast.129), channel_id=1, replica_groups=mesh['slab'=64,'head'=4] {'head'}, dimensions={0} | all-to-all | bytes 1179648 | tf_op jit(solution)/shard_map/all_to_all | solution.py:94
  (130 shorter events, 89.7 us)
Async XLA Ops:
  0.0 524.2 %copy-start = (s32[24,3]{0,1:T(4,128)S(1)}, s32[24,3]{0,1:T(4,128)}, u32[]{:S(2)}) copy-start(s32[24,3]{0,1:T(4,128)} %param.11) | copy-start | bytes 868
  1.9 499.3 %copy-start.2 = (bf16[96,3072]{1,0:T(8,128)(2,1)S(1)}, bf16[96,3072]{1,0:T(8,128)(2,1)}, u32[]{:S(2)}) copy-start(bf16[96,3072]{1,0:T(8,128)(2,1)} %param.8) | copy-start | bytes 1769476
  1.9 13.1 %all-to-all-start.1 = ((bf16[96,4,768]{2,0,1:T(8,128)(2,1)}), bf16[96,4,768]{2,0,1:T(8,128)(2,1)S(1)}, u32[]{:S(2)}, u32[]{:S(2)}) async-start(bf16[96,4,768]{2,0,1:T(8,128)(2,1)} %bitcast.73), calls=%async_computation.1 | async-start | bytes 1179648 | tf_op jit(solution)/shard_map/all_to_all | solution.py:51
  27.1 29.2 %collective-permute-start = (bf16[2,384,768]{2,1,0:T(8,128)(2,1)S(1)}, bf16[2,384,768]{2,1,0:T(8,128)(2,1)S(1)}, u32[]{:S(2)}, u32[]{:S(2)}) collective-permute-start(bf16[2,384,768]{2,1,0:T(8,128)(2,1)S(1)} %get-tuple-element.475), channel_id=1, source_target_pairs={{0,128},{128,0},{4,132},{132,4},{8,136},{136,8},{12,140},{140,12},... | collective-permute-start | bytes 3538952 | tf_op jit(solution)/shard_map/ppermute | solution.py:19
  58.1 230.8 %collective-permute-start.6 = (bf16[2,2,384,768]{3,2,1,0:T(8,128)(2,1)}, bf16[2,2,384,768]{3,2,1,0:T(8,128)(2,1)}, u32[]{:S(2)}, u32[]{:S(2)}) collective-permute-start(bf16[2,2,384,768]{3,2,1,0:T(8,128)(2,1)} %get-tuple-element.473), channel_id=1, source_target_pairs={{28,0},{32,4},{36,8},{40,12},{44,16},{48,20},{52,24},{56,28},{60,3... | collective-permute-start | bytes 7077896 | tf_op jit(solution)/shard_map/ppermute | solution.py:25
  62.3 228.5 %collective-permute-start.7 = (bf16[2,2,384,768]{3,2,1,0:T(8,128)(2,1)}, bf16[2,2,384,768]{3,2,1,0:T(8,128)(2,1)}, u32[]{:S(2)}, u32[]{:S(2)}) collective-permute-start(bf16[2,2,384,768]{3,2,1,0:T(8,128)(2,1)} %get-tuple-element.473), channel_id=1, source_target_pairs={{32,0},{36,4},{40,8},{44,12},{48,16},{52,20},{56,24},{60,28},{64,3... | collective-permute-start | bytes 7077896 | tf_op jit(solution)/shard_map/ppermute | solution.py:25
  70.5 428.8 %collective-permute-start.8 = (bf16[2,2,384,768]{3,2,1,0:T(8,128)(2,1)}, bf16[2,2,384,768]{3,2,1,0:T(8,128)(2,1)}, u32[]{:S(2)}, u32[]{:S(2)}) collective-permute-start(bf16[2,2,384,768]{3,2,1,0:T(8,128)(2,1)} %get-tuple-element.473), channel_id=1, source_target_pairs={{36,0},{40,4},{44,8},{48,12},{52,16},{56,20},{60,24},{64,28},{68,3... | collective-permute-start | bytes 7077896 | tf_op jit(solution)/shard_map/ppermute | solution.py:25
  72.4 455.8 %collective-permute-start.4 = (bf16[2,2,384,768]{3,2,1,0:T(8,128)(2,1)}, bf16[2,2,384,768]{3,2,1,0:T(8,128)(2,1)}, u32[]{:S(2)}, u32[]{:S(2)}) collective-permute-start(bf16[2,2,384,768]{3,2,1,0:T(8,128)(2,1)} %get-tuple-element.473), channel_id=1, source_target_pairs={{0,4},{4,8},{8,12},{12,16},{16,20},{20,24},{24,28},{28,32},{32,36}... | collective-permute-start | bytes 7077896 | tf_op jit(solution)/shard_map/ppermute | solution.py:25
  77.3 450.9 %collective-permute-start.5 = (bf16[2,2,384,768]{3,2,1,0:T(8,128)(2,1)}, bf16[2,2,384,768]{3,2,1,0:T(8,128)(2,1)}, u32[]{:S(2)}, u32[]{:S(2)}) collective-permute-start(bf16[2,2,384,768]{3,2,1,0:T(8,128)(2,1)} %get-tuple-element.473), channel_id=1, source_target_pairs={{4,0},{8,4},{12,8},{16,12},{20,16},{24,20},{28,24},{32,28},{36,32}... | collective-permute-start | bytes 7077896 | tf_op jit(solution)/shard_map/ppermute | solution.py:25
  288.9 488.2 %collective-permute-start.3 = (bf16[2,2,384,768]{3,2,1,0:T(8,128)(2,1)}, bf16[2,2,384,768]{3,2,1,0:T(8,128)(2,1)}, u32[]{:S(2)}, u32[]{:S(2)}) collective-permute-start(bf16[2,2,384,768]{3,2,1,0:T(8,128)(2,1)} %get-tuple-element.473), channel_id=1, source_target_pairs={{0,28},{4,32},{8,36},{12,40},{16,44},{20,48},{24,52},{28,56},{32,6... | collective-permute-start | bytes 7077896 | tf_op jit(solution)/shard_map/ppermute | solution.py:25
  290.8 509.3 %collective-permute-start.1 = (bf16[2,2,384,768]{3,2,1,0:T(8,128)(2,1)}, bf16[2,2,384,768]{3,2,1,0:T(8,128)(2,1)}, u32[]{:S(2)}, u32[]{:S(2)}) collective-permute-start(bf16[2,2,384,768]{3,2,1,0:T(8,128)(2,1)} %get-tuple-element.473), channel_id=1, source_target_pairs={{0,36},{4,40},{8,44},{12,48},{16,52},{20,56},{24,60},{28,64},{32,6... | collective-permute-start | bytes 7077896 | tf_op jit(solution)/shard_map/ppermute | solution.py:25
  499.3 300.9 %collective-permute-start.2 = (bf16[2,2,384,768]{3,2,1,0:T(8,128)(2,1)}, bf16[2,2,384,768]{3,2,1,0:T(8,128)(2,1)}, u32[]{:S(2)}, u32[]{:S(2)}) collective-permute-start(bf16[2,2,384,768]{3,2,1,0:T(8,128)(2,1)} %get-tuple-element.473), channel_id=1, source_target_pairs={{0,32},{4,36},{8,40},{12,44},{16,48},{20,52},{24,56},{28,60},{32,6... | collective-permute-start | bytes 7077896 | tf_op jit(solution)/shard_map/ppermute | solution.py:25
  502.1 308.1 %all-to-all-start = ((bf16[96,4,768]{2,0,1:T(8,128)(2,1)}), bf16[96,4,768]{2,0,1:T(8,128)(2,1)S(1)}, u32[]{:S(2)}, u32[]{:S(2)}) async-start(bf16[96,4,768]{2,0,1:T(8,128)(2,1)} %bitcast.74), calls=%async_computation | async-start | bytes 1179648 | tf_op jit(solution)/shard_map/all_to_all | solution.py:50
  800.2 10.1 %copy-start.3 = (pred[6912]{0:T(1024)(128)(4,1)S(1)}, pred[6912]{0:T(1024)(128)(4,1)}, u32[]{:S(2)}) copy-start(pred[6912]{0:T(1024)(128)(4,1)} %constant.496) | copy-start | bytes 20740
  800.2 10.1 %copy-start.4 = (pred[6912]{0:T(1024)(128)(4,1)S(1)}, pred[6912]{0:T(1024)(128)(4,1)}, u32[]{:S(2)}) copy-start(pred[6912]{0:T(1024)(128)(4,1)} %constant.497) | copy-start | bytes 20740
  800.2 10.1 %copy-start.5 = (pred[6912]{0:T(1024)(128)(4,1)S(1)}, pred[6912]{0:T(1024)(128)(4,1)}, u32[]{:S(2)}) copy-start(pred[6912]{0:T(1024)(128)(4,1)} %constant.498) | copy-start | bytes 20740
  800.2 10.1 %copy-start.6 = (pred[6912]{0:T(1024)(128)(4,1)S(1)}, pred[6912]{0:T(1024)(128)(4,1)}, u32[]{:S(2)}) copy-start(pred[6912]{0:T(1024)(128)(4,1)} %constant.499) | copy-start | bytes 20740
  800.2 10.1 %copy-start.7 = (pred[6912]{0:T(1024)(128)(4,1)S(1)}, pred[6912]{0:T(1024)(128)(4,1)}, u32[]{:S(2)}) copy-start(pred[6912]{0:T(1024)(128)(4,1)} %constant.500) | copy-start | bytes 20740
  800.2 10.1 %copy-start.8 = (pred[6912]{0:T(1024)(128)(4,1)S(1)}, pred[6912]{0:T(1024)(128)(4,1)}, u32[]{:S(2)}) copy-start(pred[6912]{0:T(1024)(128)(4,1)} %constant.501) | copy-start | bytes 20740
  800.2 10.1 %copy-start.9 = (pred[6912]{0:T(1024)(128)(4,1)S(1)}, pred[6912]{0:T(1024)(128)(4,1)}, u32[]{:S(2)}) copy-start(pred[6912]{0:T(1024)(128)(4,1)} %constant.502) | copy-start | bytes 20740
  800.2 10.1 %copy-start.10 = (pred[6912]{0:T(1024)(128)(4,1)S(1)}, pred[6912]{0:T(1024)(128)(4,1)}, u32[]{:S(2)}) copy-start(pred[6912]{0:T(1024)(128)(4,1)} %constant.503) | copy-start | bytes 20740
  800.2 10.1 %copy-start.11 = (pred[6912]{0:T(1024)(128)(4,1)S(1)}, pred[6912]{0:T(1024)(128)(4,1)}, u32[]{:S(2)}) copy-start(pred[6912]{0:T(1024)(128)(4,1)} %constant.504) | copy-start | bytes 20740
  800.2 10.1 %copy-start.12 = (pred[6912]{0:T(1024)(128)(4,1)S(1)}, pred[6912]{0:T(1024)(128)(4,1)}, u32[]{:S(2)}) copy-start(pred[6912]{0:T(1024)(128)(4,1)} %constant.505) | copy-start | bytes 20740
  950.3 51.9 %copy-start.1 = (s32[24,3]{0,1:T(4,128)S(1)}, s32[24,3]{0,1:T(4,128)}, u32[]{:S(2)}) copy-start(s32[24,3]{0,1:T(4,128)} %param.11) | copy-start | bytes 868
  (7 other events, 70.5 us)
where the time goes:
time: 1000 us
  waiting for transfers between devices  582 us (58%)
  starting transfers between devices  193 us (19%)
  other arithmetic  109 us (11%)
  blocking collectives  63 us (6%)
  local copies, waits for them, and re-layouts  29 us (3%)
  matrix products  25.5 us (3%)
    ppermute x8, waiting for transfers between devices, from_behind(): return lax.ppermute(value, axis, pairs)  547 us
    ppermute x8, starting transfers between devices, from_behind(): return lax.ppermute(value, axis, pairs)  165 us
    gather x6, other arithmetic, one_head(): keep = jnp.repeat(allowed, tile, total_repeat_length=18 * tile)  68.1 us
    all_to_all x1, blocking collectives, shards(): lax.all_to_all(result, 'head', split_axis=0, concat_axis=1, tiled=True)  51 us
    ppermute x1, waiting for transfers between devices, from_partner(): return lax.ppermute(block, axis, route)  27 us
    all_to_all x1, starting transfers between devices, shards(): lax.all_to_all(queries, 'head', split_axis=1, concat_axis=0, tiled=True)  22.1 us
  transfers between devices with their start and end apart: 11, of which 6 were waited for; matrix products, arithmetic and copies ran while one was open for 2% of the time, Pallas kernels for 0%

commit v1 on v0

v1 whole, which is shorter than its diff:
```python
import functools

import jax
import jax.numpy as jnp
from jax import lax
from jax.experimental import pallas as pl
from jax.experimental.pallas import tpu as pltpu
from jax.sharding import PartitionSpec as P

MESH = pl.DeviceIdType.MESH
ANY = pl.BlockSpec(memory_space=pl.ANY)
SMEM = pl.BlockSpec(memory_space=pltpu.SMEM)
VMEM = pl.BlockSpec(memory_space=pltpu.VMEM)
HEADS, HD, TILE, PART = 24, 128, 384, 96
SLOTS, CHIPS = 3, 8
LOG2E = 1.4426950408889634


def coords():
    slab, head = lax.axis_index("slab"), lax.axis_index("head")
    x, z, y_hi = slab // 16, (slab // 2) % 8, slab % 2
    return x, y_hi * 2 + head // 2, z, head % 2


def device(x, y, z, c):
    return ((x * 8 + z) * 2 + y // 2, (y % 2) * 2 + c)


def remote(src, dst, send, recv, to):
    return pltpu.make_async_remote_copy(
        src_ref=src, dst_ref=dst, send_sem=send, recv_sem=recv, device_id=to, device_id_type=MESH
    )


def greet(devices):
    barrier = pltpu.get_barrier_semaphore()
    for to in devices:
        pl.semaphore_signal(barrier, 1, device_id=to, device_id_type=MESH)
    pl.semaphore_wait(barrier, len(devices))


def group(x, y, z, c):
    return [
        device((x + 2 * i) % 4, (y + m) % 4, z, (c + n) % 2)
        for i in range(2)
        for m in range(4)
        for n in range(2)
        if (i, m, n) != (0, 0, 0)
    ]


def pack_kernel(rank, q_in, k_in, v_in, q_out, kv_out):
    for e in range(HEADS):
        r = rank[e]
        cols = pl.ds(e * HD, HD)
        q_out[r] = q_in[:, cols]
        kv_out[r, 0] = k_in[:, cols]
        kv_out[r, 1] = v_in[:, cols]


def unpack_kernel(rank, o_in, out):
    for e in range(HEADS):
        out[:, e * HD : (e + 1) * HD] = o_in[rank[e]]


def gather_kernel(
    far, qh, kvh, q, kv, relay, a_send, q_send, kv_recv, q_recv, hop_send, hop_recv, own_send, own_recv,
    mid_send, mid_recv, x_send, x_recv, xs_send, xs_recv,
):
    x, y, z, c = coords()
    z_hi, x_lo, t = z // 4, x % 2, x // 2
    up, down = (z + 1) % 8, (z + 7) % 8
    twin = device(x, y, z, 1 - c)
    side = device(x + 1 - 2 * x_lo, y, z, c)
    ahead = device(x, y, jnp.where(c == 0, up, down), c)
    first = device(x, y, jnp.where(c == 0, down, up), 1 - c)
    greet(
        group(x, y, z, c)
        + [device(x, y, up, c), device(x, y, up, 1 - c), device(x, y, down, c), device(x, y, down, 1 - c), side]
    )

    y_hi = y // 2
    part = (y % 2) * 2 + c
    me = t * 4 + y
    rows = pl.ds(part * PART, PART)
    copies = []

    def send(src, dst, sem, recv, chip):
        alone = (chip == me) & (c == y_hi)
        to = device((chip // 4) * 2 + x_lo, chip % 4, z, y_hi)

        @pl.when(alone)
        def _():
            pltpu.make_async_copy(src, dst, recv).start()

        @pl.when(jnp.logical_not(alone))
        def _():
            remote(src, dst, sem, recv, to).start()

        copies.append((alone, remote(src, dst, sem, recv, to)))

    for k in range(SLOTS):
        for i in range(CHIPS):
            chip = (me + i) % CHIPS
            send(kvh.at[k, chip], kv.at[k, 1, 1, :, t, rows], a_send.at[k, i], kv_recv.at[k], chip)
    for i in range(CHIPS):
        chip = (me + i) % CHIPS
        send(qh.at[:, chip], q.at[:, t, rows], q_send.at[i], q_recv, chip)

    outer = c * 2
    inner = 2 - outer
    near = 2 - 2 * z_hi
    z_next = jnp.where(c == 0, up, down)
    near_next = 2 - 2 * (z_next // 4)
    started = []

    def go(copy):
        copy.start()
        started.append(copy)

    def landing(k, hop, part, near_of):
        if hop == 1:
            return kv.at[k, 1, outer, part]
        if hop < 4:
            return relay.at[k, hop - 2, part]
        return kv.at[k, near_of, inner if hop == 4 else outer, part]

    def hop_wait(k, hop, part):
        place = landing(k, hop, part, near)
        pltpu.make_async_copy(place, place, hop_recv.at[k, hop - 1, part]).wait()

    def wait_for(place, sem):
        pltpu.make_async_copy(place, place, sem).wait()

    def begin(k):
        own = kv.at[k, 1, 1]
        wait_for(own, kv_recv.at[k])
        for part in range(2):
            go(remote(kv.at[k, 1, 1, part], kv.at[k, 1, inner, part], hop_send.at[k, 0, part], hop_recv.at[k, 0, part], first))
        go(remote(own, kv.at[k, 1, outer], own_send.at[k], own_recv.at[k], twin))

    def forward(k, hop):
        for part in range(2):
            hop_wait(k, hop - 1, part)
            go(
                remote(
                    landing(k, hop - 1, part, near),
                    landing(k, hop, part, near_next),
                    hop_send.at[k, hop - 1, part],
                    hop_recv.at[k, hop - 1, part],
                    ahead,
                )
            )

    sender = x_lo == z_hi
    side_copies = []

    def aside(k, n, place):
        copy = remote(kv.at[k, near, place], kv.at[k, 2 - near, place], x_send.at[k, n], x_recv.at[k, n], side)
        side_copies.append(copy)
        pl.when(sender)(copy.start)

    def middle(k):
        go(remote(kv.at[k, near, inner], kv.at[k, near, 1], mid_send.at[k], mid_recv.at[k], twin))
        aside(k, 0, inner)

    def finish(k):
        for part in range(2):
            hop_wait(k, 5, part)
        aside(k, 1, outer)

    def side_share(k):
        share = remote(kv.at[k, 2 - near, inner], kv.at[k, 2 - near, 1], xs_send.at[k], xs_recv.at[k], twin)
        side_copies.append(share)

        @pl.when(jnp.logical_not(sender))
        def _():
            wait_for(kv.at[k, 2 - near, inner], x_recv.at[k, 0])
            share.start()

    begin(0)
    begin(1)
    for k in range(far):
        forward(k, 2)
        if k > 0:
            finish(k - 1)
        forward(k, 3)
        if k == 0:
            begin(2)
        forward(k, 4)
        if k > 0:
            side_share(k - 1)
        forward(k, 5)
        middle(k)
    if far == 0:
        begin(2)
    else:
        finish(far - 1)
        side_share(far - 1)

    for k in range(SLOTS):
        if k >= far:
            for part in range(2):
                hop_wait(k, 1, part)
        else:
            wait_for(kv.at[k, near, 1], mid_recv.at[k])
        wait_for(kv.at[k, 1, inner], own_recv.at[k])
    wait_for(q, q_recv)
    for alone, copy in copies:
        pl.when(jnp.logical_not(alone))(copy.wait_send)
    for copy in started:
        copy.wait_send()
    for k in range(far):

        @pl.when(sender)
        def _():
            for n in range(2):
                place = kv.at[k, near, inner if n == 0 else outer]
                remote(place, place, x_send.at[k, n], x_recv.at[k, n], side).wait_send()

        @pl.when(jnp.logical_not(sender))
        def _():
            place = kv.at[k, 2 - near, inner]
            remote(place, place, xs_send.at[k], xs_recv.at[k], twin).wait_send()
            wait_for(kv.at[k, 2 - near, outer], x_recv.at[k, 1])
            wait_for(kv.at[k, 2 - near, 1], xs_recv.at[k])


def gather(far, qh, kvh):
    dma = pltpu.SemaphoreType.DMA
    return pl.pallas_call(
        functools.partial(gather_kernel, far),
        out_shape=(
            jax.ShapeDtypeStruct((SLOTS, 2, TILE, HD), jnp.bfloat16),
            jax.ShapeDtypeStruct((SLOTS, 3, 3, 2, 2, TILE, HD), jnp.bfloat16),
        ),
        in_specs=[ANY, ANY],
        out_specs=(ANY, ANY),
        scratch_shapes=[
            pltpu.VMEM((SLOTS, 2, 2, 2, TILE, HD), jnp.bfloat16),
            dma((SLOTS, CHIPS)),
            dma((CHIPS,)),
            dma((SLOTS,)),
            dma,
            dma((SLOTS, 5, 2)),
            dma((SLOTS, 5, 2)),
            dma((SLOTS,)),
            dma((SLOTS,)),
            dma((SLOTS,)),
            dma((SLOTS,)),
            dma((SLOTS, 2)),
            dma((SLOTS, 2)),
            dma((SLOTS,)),
            dma((SLOTS,)),
        ],
        compiler_params=pltpu.CompilerParams(collective_id=far, has_side_effects=True, vmem_limit_bytes=32 << 20),
        name=f"gather{far}",
    )(qh, kvh)


def attend_kernel(reach, q_hbm, kv_hbm, out, q, kv, q_sem, kv_sem, top, total, acc):
    x, y, z, c = coords()
    h, w = (x % 2) * 2 + z // 4, (z % 4) * 2 + c
    chip = (x // 2) * 4 + y
    load_q = pltpu.make_async_copy(q_hbm, q, q_sem)
    load_q.start()
    order = [(1, 1), (1, 0), (1, 2), (0, 1), (0, 0), (0, 2), (2, 1), (2, 0), (2, 2)]

    def allowed(k, dh, dw):
        row = k * CHIPS + chip
        ok_h = (dh == 1) | ((reach[row, 1] > 0) & (h + dh - 1 >= 0) & (h + dh - 1 < 4))
        ok_w = (dw == 1) | ((reach[row, 2] > 0) & (w + dw - 1 >= 0) & (w + dw - 1 < 8))
        return ok_h & ok_w

    def load(k, dh, dw):
        return pltpu.make_async_copy(kv_hbm.at[k, dh, dw], kv.at[k, dh, dw], kv_sem.at[k, dh, dw])

    for k in range(SLOTS):
        for dh, dw in order:
            pl.when(allowed(k, dh, dw))(load(k, dh, dw).start)
    load_q.wait()
    scale = HD ** (-0.5) * LOG2E
    QB = 128

    def update(k, t, keys, vals):
        for b in range(TILE // QB):
            rows = pl.ds(t * TILE + b * QB, QB)
            query = q[k, t, b * QB : (b + 1) * QB]
            s = lax.dot_general(query, keys, (((1,), (1,)), ((), ())), preferred_element_type=jnp.float32)
            old = top[rows]
            new = jnp.maximum(old, jnp.max(s, axis=1, keepdims=True))
            p = jnp.exp2(s * scale - new[:, :1] * scale)
            fix = jnp.exp2((old - new) * scale)
            total[rows] = total[rows] * fix + jnp.sum(p, axis=1, keepdims=True)
            acc[rows] = acc[rows] * fix + jnp.dot(p.astype(jnp.bfloat16), vals, preferred_element_type=jnp.float32)
            top[rows] = new

    def one_head(k, carry):
        top[...] = jnp.full_like(top, -1e30)
        total[...] = jnp.zeros_like(total)
        acc[...] = jnp.zeros_like(acc)
        both = reach[k * CHIPS + chip, 0] > 0

        def one_tile(n, carry):
            dh, dw = (n // 3 + 1) % 3, (n % 3 + 1) % 3

            @pl.when(allowed(k, dh, dw))
            def _():
                load(k, dh, dw).wait()

                @pl.when(both)
                def _():
                    keys = kv[k, dh, dw, 0].reshape(2 * TILE, HD)
                    vals = kv[k, dh, dw, 1].reshape(2 * TILE, HD)
                    for t in range(2):
                        update(k, t, keys, vals)

                @pl.when(jnp.logical_not(both))
                def _():
                    for t in range(2):
                        update(k, t, kv[k, dh, dw, 0, t], kv[k, dh, dw, 1, t])

            return carry

        lax.fori_loop(0, 9, one_tile, 0)
        result = acc[...] / total[...]
        out[k] = result.astype(jnp.bfloat16).reshape(2, TILE, HD)
        return carry

    lax.fori_loop(0, SLOTS, one_head, 0)


def attend(reach, q, kv):
    dma = pltpu.SemaphoreType.DMA
    return pl.pallas_call(
        attend_kernel,
        out_shape=jax.ShapeDtypeStruct((SLOTS, 2, TILE, HD), jnp.bfloat16),
        in_specs=[SMEM, ANY, ANY],
        out_specs=VMEM,
        scratch_shapes=[
            pltpu.VMEM((SLOTS, 2, TILE, HD), jnp.bfloat16),
            pltpu.VMEM((SLOTS, 3, 3, 2, 2, TILE, HD), jnp.bfloat16),
            dma,
            dma((SLOTS, 3, 3)),
            pltpu.VMEM((2 * TILE, HD), jnp.float32),
            pltpu.VMEM((2 * TILE, HD), jnp.float32),
            pltpu.VMEM((2 * TILE, HD), jnp.float32),
        ],
        compiler_params=pltpu.CompilerParams(vmem_limit_bytes=40 << 20),
        name="attend",
    )(reach, q, kv)


def return_kernel(o, back, send_sem, recv_sem):
    x, y, z, c = coords()
    x_lo = x % 2
    chip = (x // 2) * 4 + y
    greet(group(x, y, z, c))
    mine = (x // 2) * 4 + (y % 2) * 2 + c
    home = y // 2 == c
    copies = []
    for i in range(8):
        n = (mine + i) % 8
        t, part = n // 4, n % 4
        to = device(t * 2 + x_lo, c * 2 + part // 2, z, part % 2)
        src = o.at[:, t, pl.ds(part * PART, PART)]
        dst = back.at[:, chip]
        copy = remote(src, dst, send_sem.at[i], recv_sem, to)
        if i == 0:
            pl.when(home)(pltpu.make_async_copy(src, dst, recv_sem).start)
            pl.when(jnp.logical_not(home))(copy.start)
        else:
            copy.start()
        copies.append(copy)
    pltpu.make_async_copy(back, back, recv_sem).wait()
    for i, copy in enumerate(copies):
        if i == 0:
            pl.when(jnp.logical_not(home))(copy.wait_send)
        else:
            copy.wait_send()


def give_back(o):
    dma = pltpu.SemaphoreType.DMA
    return pl.pallas_call(
        return_kernel,
        out_shape=jax.ShapeDtypeStruct((SLOTS, CHIPS, PART, HD), jnp.bfloat16),
        in_specs=[ANY],
        out_specs=ANY,
        scratch_shapes=[dma((8,)), dma],
        compiler_params=pltpu.CompilerParams(collective_id=8, has_side_effects=True),
        name="give_back",
    )(o)


def shards(queries, keys, values, windows):
    weight = windows[:, 1] * 4 + windows[:, 2] * 2 + windows[:, 0]
    index = jnp.arange(HEADS, dtype=jnp.int32)
    ahead = (weight[None, :] > weight[:, None]) | ((weight[None, :] == weight[:, None]) & (index[None, :] < index[:, None]))
    rank = jnp.sum(ahead.astype(jnp.int32), axis=1)
    rank = jnp.where(rank // CHIPS == 1, 3 * CHIPS - 1 - rank, rank)
    reach = jnp.sum(jnp.where(rank[None, :, None] == index[:, None, None], windows[None], 0), axis=1)
    far = (jnp.sum(windows[:, 1]) + CHIPS - 1) // CHIPS

    qh, kvh = pl.pallas_call(
        pack_kernel,
        out_shape=(
            jax.ShapeDtypeStruct((HEADS, PART, HD), jnp.bfloat16),
            jax.ShapeDtypeStruct((HEADS, 2, PART, HD), jnp.bfloat16),
        ),
        in_specs=[SMEM, VMEM, VMEM, VMEM],
        out_specs=(VMEM, VMEM),
        name="pack",
    )(rank, queries, keys, values)
    qh = qh.reshape(SLOTS, CHIPS, PART, HD)
    kvh = kvh.reshape(SLOTS, CHIPS, 2, PART, HD)

    def branch(n):
        def run(qh, kvh, reach):
            q, kv = gather(n, qh, kvh)
            return attend(reach, q, kv)

        return run

    o = lax.switch(far, [branch(n) for n in range(SLOTS + 1)], qh, kvh, reach)
    back = give_back(o)
    return pl.pallas_call(
        unpack_kernel,
        out_shape=jax.ShapeDtypeStruct((PART, HEADS * HD), jnp.bfloat16),
        in_specs=[SMEM, VMEM],
        out_specs=VMEM,
        name="unpack",
    )(rank, back.reshape(HEADS, PART, HD))


def solution(mesh):
    tokens = P(("slab", "head"), None)
    return jax.shard_map(
        shards, mesh=mesh, in_specs=(tokens, tokens, tokens, P()), out_specs=tokens, check_vma=False
    )
```

time: 1000 us -> 150 us (0.15)
  the two profiles are of different devices: /device:TPU:162 before, /device:TPU:7 now
where the time goes in v1:
time: 150 us; the launch traced here: 147 us
  Pallas kernels  143 us (95%)
  other arithmetic  2.46 us (2%)
    pallas_call x1, Pallas kernels, gather(): pl.pallas_call(functools.partial(gather_kernel, far), out_shape=(jax.Shap...  75.4 us
    pallas_call x1, Pallas kernels, attend(): pl.pallas_call(attend_kernel, out_shape=jax.ShapeDtypeStruct((SLOTS, 2, T...  41.3 us
    pallas_call x1, Pallas kernels, give_back(): pl.pallas_call(return_kernel, out_shape=jax.ShapeDtypeStruct((SLOTS, CHIP...  22.9 us

profile of v1, /device:TPU:7, one launch (start us, length us, event | category | flops | bytes accessed | tf_op | source)
XLA Modules:
  0.0 147.2 jit_solution(5651915610124255995)
XLA Ops:
  0.0 1.4 slice_reduce_fusion
  2.1 0.2 convert_reduce_fusion
  2.3 0.0 copy-start
  2.3 0.8 select_reduce_fusion
  3.2 0.0 copy-done
  3.2 1.7 %pack.1 = (bf16[24,96,128]{2,1,0:T(8,128)(2,1)S(1)}, bf16[24,2,96,128]{3,2,1,0:T(8,128)(2,1)S(1)}) custom-call(s32[24]{0:T(128)} %copy-done, bf16[96,3072]{1,0:T(8,128)(2,1)} %q_in.1, bf16[96,3072]{1,0:T(8,128)(2,1)} %k_in.1, bf16[96,3072]{1,0:T(8,128)(2,1)} %v_in.1), custom_call_target="tpu_custom_call" | custom-call | tf_op jit(solution)/shard_map/pack/pallas_call | solution.py:405
  4.9 117.3 %conditional.1 = (bf16[3,2,384,128]{3,2,1,0:T(8,128)(2,1)S(1)}) conditional(s32[]{:T(128)} %clamp.3, (bf16[3,8,96,128]{3,2,1,0:T(8,128)(2,1)S(1)}, bf16[3,8,2,96,128]{4,3,2,1,0:T(8,128)(2,1)S(1)}, s32[24,3]{0,1:T(4,128)S(1)}) %tuple.31, (bf16[3,8,96,128]{3,2,1,0:T(8,128)(2,1)S(1)}, ...), branch_computations={%region_3.4_spmd, %region_4.5_spmd, %region_5.6_spmd, %region_6.7_... | conditional | bytes 584 | solution.py:425
  4.9 0.1 copy.8.reach
  5.0 75.4 %gather2.1 = (bf16[3,2,384,128]{3,2,1,0:T(8,128)(2,1)S(1)}, bf16[3,3,3,2,2,384,128]{6,5,4,3,2,1,0:T(8,128)(2,1)S(1)}) custom-call(bf16[3,8,96,128]{3,2,1,0:T(8,128)(2,1)S(1)} %get-tuple-element.45.qh, bf16[3,8,2,96,128]{4,3,2,1,0:T(8,128)(2,1)S(1)} %get-tuple-element.46.kvh), custom_call_target="tpu_custom_call" | custom-call | tf_op jit(solution)/shard_map/cond/branch_2_fun/gather2/pallas_call | solution.py:231
  80.4 41.3 %attend.6 = bf16[3,2,384,128]{3,2,1,0:T(8,128)(2,1)S(1)} custom-call(s32[24,3]{1,0:T(8,128)S(1)} %copy.8.reach, bf16[3,2,384,128]{3,2,1,0:T(8,128)(2,1)S(1)} %get-tuple-element.47.q_hbm, bf16[3,3,3,2,2,384,128]{6,5,4,3,2,1,0:T(8,128)(2,1)S(1)} %get-tuple-element.48.kv_hbm), custom_call_target="tpu_custom_call" | custom-call | tf_op jit(solution)/shard_map/cond/branch_2_fun/attend/pallas_call | solution.py:335
  122.2 22.9 %give_back.1 = bf16[3,8,96,128]{3,2,1,0:T(8,128)(2,1)} custom-call(bf16[3,2,384,128]{3,2,1,0:T(8,128)(2,1)S(1)} %get-tuple-element.72.o), custom_call_target="tpu_custom_call" | custom-call | tf_op jit(solution)/shard_map/give_back/pallas_call | solution.py:385
  145.1 2.0 %unpack.1 = bf16[96,3072]{1,0:T(8,128)(2,1)} custom-call(s32[24]{0:T(128)} %copy-done, bf16[24,96,128]{2,1,0:T(8,128)(2,1)} %bitcast.13), custom_call_target="tpu_custom_call" | custom-call | tf_op jit(solution)/shard_map/unpack/pallas_call | solution.py:427
  (2 shorter events, 0.0 us)
Async XLA Ops:
  2.3 0.9 copy-start

commit v2 on v0

v2 whole, which is shorter than its diff:
```python
import functools

import jax
import jax.numpy as jnp
from jax import lax
from jax.experimental import pallas as pl
from jax.experimental.pallas import tpu as pltpu
from jax.sharding import PartitionSpec as P

MESH = pl.DeviceIdType.MESH
ANY = pl.BlockSpec(memory_space=pl.ANY)
SMEM = pl.BlockSpec(memory_space=pltpu.SMEM)
VMEM = pl.BlockSpec(memory_space=pltpu.VMEM)
HEADS, HD, TILE, PART = 24, 128, 384, 96
SLOTS, CHIPS = 3, 8
LOG2E = 1.4426950408889634


def coords():
    slab, head = lax.axis_index("slab"), lax.axis_index("head")
    x, z, y_hi = slab // 16, (slab // 2) % 8, slab % 2
    return x, y_hi * 2 + head // 2, z, head % 2


def device(x, y, z, c):
    return ((x * 8 + z) * 2 + y // 2, (y % 2) * 2 + c)


def remote(src, dst, send, recv, to):
    return pltpu.make_async_remote_copy(
        src_ref=src, dst_ref=dst, send_sem=send, recv_sem=recv, device_id=to, device_id_type=MESH
    )


def greet(devices):
    barrier = pltpu.get_barrier_semaphore()
    for to in devices:
        pl.semaphore_signal(barrier, 1, device_id=to, device_id_type=MESH)
    pl.semaphore_wait(barrier, len(devices))


def group(x, y, z, c):
    return [
        device((x + 2 * i) % 4, (y + m) % 4, z, (c + n) % 2)
        for i in range(2)
        for m in range(4)
        for n in range(2)
        if (i, m, n) != (0, 0, 0)
    ]


def pack_kernel(perm, q_in, k_in, v_in, qh, kvh):
    for r in range(HEADS):
        cols = pl.ds(pl.multiple_of(perm[r] * HD, HD), HD)
        qh[r] = q_in[:, cols]
        kvh[r, 0] = k_in[:, cols]
        kvh[r, 1] = v_in[:, cols]


def pack(perm, queries, keys, values):
    qh, kvh = pl.pallas_call(
        pack_kernel,
        out_shape=(
            jax.ShapeDtypeStruct((HEADS, PART, HD), jnp.bfloat16),
            jax.ShapeDtypeStruct((HEADS, 2, PART, HD), jnp.bfloat16),
        ),
        in_specs=[SMEM, VMEM, VMEM, VMEM],
        out_specs=(VMEM, VMEM),
        name="pack",
    )(perm, queries, keys, values)
    return qh.reshape(SLOTS, CHIPS, PART, HD), kvh.reshape(SLOTS, CHIPS, 2, PART, HD)


def plan(far):
    main = [("begin", 0)]
    for k in range(far):
        for hop in range(2, 6):
            for part in range(2):
                main.append(("forward", k, hop, part))
            if k == 0 and hop == 2:
                main.append(("begin", 1))
            if k == 0 and hop == 5:
                main.append(("begin", 2))
            if k > 0 and hop == 2:
                main.append(("finish", k - 1))
            if k > 0 and hop == 4:
                main.append(("share", k - 1))
    if far == 0:
        main += [("begin", 1), ("begin", 2)]
    else:
        main += [("finish", far - 1), ("share", far - 1)]

    def ready(event):
        if event[0] == "begin":
            k = event[1]
            return [(0, k, "own"), (1, k, "inner")] + ([] if k < far else [(3, k, "outer")])
        if event[0] == "forward":
            k, hop, part = event[1:]
            if part == 1 and hop == 2:
                return [(0, k, "outer")]
            if part == 1 and hop == 5:
                return [(0, k, "near inner"), (1, k, "near own")]
            return []
        if event[0] == "finish":
            return [(0, event[1], "near outer")]
        return [(0, event[1], "side inner"), (1, event[1], "side own"), (4, event[1], "side outer")]

    steps, pool = [], []
    n = 0
    while n < len(main) or pool:
        events = []
        if n < len(main):
            events.append(main[n])
            pool += [(n + late, len(pool), k, what) for late, k, what in ready(main[n])]
        pool.sort(key=lambda p: p[0])
        pick = None
        if pool and (pool[0][0] <= n or n >= len(main)):
            pick = pool.pop(0)[2:]
        steps.append((events, pick))
        n += 1
    return steps


PLACES = ["own", "inner", "outer", "near own", "near inner", "near outer", "side own", "side inner", "side outer"]


def kernel(
    far, rank, barred, qh, kvh, out,
    q, kv, relay, vt, top, acc, o, back,
    a_send, q_send, kv_recv, q_recv, hop_send, hop_recv, own_send, own_recv,
    mid_send, mid_recv, x_send, x_recv, xs_send, xs_recv, o_send, o_recv,
):
    x, y, z, c = coords()
    z_hi, x_lo, t = z // 4, x % 2, x // 2
    up, down = (z + 1) % 8, (z + 7) % 8
    twin = device(x, y, z, 1 - c)
    side = device(x + 1 - 2 * x_lo, y, z, c)
    ahead = device(x, y, jnp.where(c == 0, up, down), c)
    first = device(x, y, jnp.where(c == 0, down, up), 1 - c)
    barrier = pltpu.get_barrier_semaphore()
    partners = group(x, y, z, c) + [
        device(x, y, up, c), device(x, y, up, 1 - c), device(x, y, down, c), device(x, y, down, 1 - c), side
    ]
    for to in partners:
        pl.semaphore_signal(barrier, 1, device_id=to, device_id_type=MESH)

    pl.semaphore_wait(barrier, len(partners))

    y_hi = y // 2
    part = (y % 2) * 2 + c
    me = t * 4 + y
    rows = pl.ds(part * PART, PART)
    copies = []

    def send(src, dst, sem, recv, chip):
        alone = (chip == me) & (c == y_hi)
        to = device((chip // 4) * 2 + x_lo, chip % 4, z, y_hi)

        @pl.when(alone)
        def _():
            pltpu.make_async_copy(src, dst, recv).start()

        @pl.when(jnp.logical_not(alone))
        def _():
            remote(src, dst, sem, recv, to).start()

        copies.append((alone, remote(src, dst, sem, recv, to)))

    def scatter(k):
        for i in range(CHIPS):
            chip = (me + i) % CHIPS
            send(kvh.at[k, chip], kv.at[k, 1, 1, :, t, rows], a_send.at[k, i], kv_recv.at[k], chip)

    scatter(0)
    for i in range(CHIPS):
        chip = (me + i) % CHIPS
        send(qh.at[:, chip], q.at[:, t, rows], q_send.at[i], q_recv, chip)
    scatter(1)
    scatter(2)
    top[...] = jnp.full_like(top, -1e30)
    acc[...] = jnp.zeros_like(acc)
    vt[HD:] = jnp.ones((16, 2 * TILE), jnp.bfloat16)

    outer = c * 2
    inner = 2 - outer
    near = 2 - 2 * z_hi
    z_next = jnp.where(c == 0, up, down)
    near_next = 2 - 2 * (z_next // 4)
    sender = x_lo == z_hi
    receiver = jnp.logical_not(sender)
    w_edge = jnp.where(c == 0, z % 4 > 0, z % 4 < 3)

    def wait_for(place, sem):
        pltpu.make_async_copy(place, place, sem).wait()

    def landing(k, hop, part, near_of):
        if hop == 1:
            return kv.at[k, 1, outer, part]
        if hop < 4:
            return relay.at[k, hop - 2, part]
        return kv.at[k, near_of, inner if hop == 4 else outer, part]

    def hop_wait(k, hop, part):
        wait_for(landing(k, hop, part, near), hop_recv.at[k, hop - 1, part])

    def first_hop(k, part):
        return remote(
            kv.at[k, 1, 1, part], kv.at[k, 1, inner, part], hop_send.at[k, 0, part], hop_recv.at[k, 0, part], first
        )

    def next_hop(k, hop, part):
        return remote(
            landing(k, hop - 1, part, near),
            landing(k, hop, part, near_next),
            hop_send.at[k, hop - 1, part],
            hop_recv.at[k, hop - 1, part],
            ahead,
        )

    def own_share(k):
        return remote(kv.at[k, 1, 1], kv.at[k, 1, outer], own_send.at[k], own_recv.at[k], twin)

    def mid_share(k):
        return remote(kv.at[k, near, inner], kv.at[k, near, 1], mid_send.at[k], mid_recv.at[k], twin)

    def aside(k, n):
        place = inner if n == 0 else outer
        return remote(kv.at[k, near, place], kv.at[k, 2 - near, place], x_send.at[k, n], x_recv.at[k, n], side)

    def side_share(k):
        return remote(kv.at[k, 2 - near, inner], kv.at[k, 2 - near, 1], xs_send.at[k], xs_recv.at[k], twin)

    def give_back(k, i):
        n = (t * 4 + part + i) % 8
        to = device((n // 4) * 2 + x_lo, c * 2 + (n % 4) // 2, z, n % 2)
        src = o.at[k, n // 4, pl.ds((n % 4) * PART, PART)]
        dst = back.at[k * CHIPS + me]
        return src, dst, remote(src, dst, o_send.at[k, i], o_recv.at[k], to)

    def communicate(event):
        what, k = event[0], event[1]
        if what == "begin":
            wait_for(kv.at[k, 1, 1], kv_recv.at[k])
            for part in range(2):
                first_hop(k, part).start()
            own_share(k).start()
            if k == 0:
                wait_for(q, q_recv)
        elif what == "forward":
            hop, part = event[2:]
            hop_wait(k, hop - 1, part)
            next_hop(k, hop, part).start()
            if hop == 5 and part == 1:
                mid_share(k).start()
                pl.when(sender)(aside(k, 0).start)
        elif what == "finish":
            for part in range(2):
                hop_wait(k, 5, part)
            pl.when(sender)(aside(k, 1).start)
        else:

            @pl.when(receiver)
            def _():
                wait_for(kv.at[k, 2 - near, inner], x_recv.at[k, 0])
                side_share(k).start()

    def arrive(k, what):
        if what == "inner":
            wait_for(kv.at[k, 1, inner], own_recv.at[k])
        elif what == "outer" and k >= far:
            for part in range(2):
                hop_wait(k, 1, part)
        elif what == "near own":
            wait_for(kv.at[k, near, 1], mid_recv.at[k])
        elif what == "side own":
            pl.when(receiver)(lambda: wait_for(kv.at[k, 2 - near, 1], xs_recv.at[k]))
        elif what == "side outer":
            pl.when(receiver)(lambda: wait_for(kv.at[k, 2 - near, outer], x_recv.at[k, 1]))

    scale = HD ** (-0.5) * LOG2E

    def attention(k, place):
        dh, dw = place // 3, place % 3
        row = k * CHIPS + me
        row_at = jnp.where(dh == 0, 1, jnp.where(dh == 1, near, 2 - near))
        col_at = jnp.where(dw == 0, 1, jnp.where(dw == 1, inner, outer))
        off = barred[row, 1] * jnp.minimum(dh, 1).astype(jnp.float32)
        off += barred[row, 2] * jnp.minimum(dw, 1).astype(jnp.float32)
        off += jnp.where((dw == 2) & jnp.logical_not(w_edge), 1e30, 0.0)
        off_time = off + barred[row, 0]
        tile = kv.at[k, row_at, col_at]
        vt[:HD] = tile[1].reshape(2 * TILE, HD).T
        scores = [
            [
                lax.dot_general(tile[0, u], q[k, s], (((1,), (1,)), ((), ())), preferred_element_type=jnp.float32)
                for u in range(2)
            ]
            for s in range(2)
        ]
        for s in range(2):
            old = top[k, s, :1]
            new = old
            for u in range(2):
                best = jnp.max(scores[s][u], axis=0, keepdims=True)
                new = jnp.maximum(new, best - (off if u == s else off_time))
            p = [
                jnp.exp2((scores[s][u] - (new + (off if u == s else off_time))) * scale).astype(jnp.bfloat16)
                for u in range(2)
            ]
            fix = jnp.exp2((old - new) * scale)
            add = jnp.dot(vt[...], jnp.concatenate(p, axis=0), preferred_element_type=jnp.float32)
            acc[k, s] = acc[k, s] * fix + add
            top[k, s] = jnp.broadcast_to(new, (8, TILE))

    def conclude(k):
        for s in range(2):
            o[k, s] = (acc[k, s, :HD] / acc[k, s, HD : HD + 1]).T.astype(jnp.bfloat16)
        for i in range(8):
            src, dst, copy = give_back(k, i)
            if i == 0:
                pl.when(y_hi == c)(pltpu.make_async_copy(src, dst, o_recv.at[k]).start)
                pl.when(y_hi != c)(copy.start)
            else:
                copy.start()

    steps = plan(far)
    last = {}
    for n, (events, pick) in enumerate(steps):
        if pick:
            last[pick[0]] = n

    def one_step(n, carry):
        code = jnp.int32(-1)
        for m, (events, pick) in enumerate(steps):

            @pl.when(n == m)
            def _():
                for event in events:
                    communicate(event)
                if pick:
                    arrive(*pick)

            if pick:
                code = jnp.where(n == m, pick[0] * 9 + PLACES.index(pick[1]), code)

        @pl.when((code >= 0) & ((code % 9 < 6) | receiver))
        def _():
            attention(code // 9, code % 9)

        for k in range(SLOTS):
            pl.when(n == last[k])(lambda: conclude(k))
        return carry

    lax.fori_loop(0, len(steps), one_step, 0)

    for k in range(SLOTS):
        wait_for(back.at[pl.ds(k * CHIPS, CHIPS)], o_recv.at[k])
    for e in range(HEADS):
        out[:, e * HD : (e + 1) * HD] = back[rank[e]]

    for alone, copy in copies:
        pl.when(jnp.logical_not(alone))(copy.wait_send)
    for k in range(SLOTS):
        for part_ in range(2):
            first_hop(k, part_).wait_send()
        own_share(k).wait_send()
        for i in range(8):
            copy = give_back(k, i)[2]
            if i == 0:
                pl.when(y_hi != c)(copy.wait_send)
            else:
                copy.wait_send()
    for k in range(far):
        for hop in range(2, 6):
            for part_ in range(2):
                next_hop(k, hop, part_).wait_send()
        mid_share(k).wait_send()
        for n in range(2):
            pl.when(sender)(aside(k, n).wait_send)
        pl.when(receiver)(side_share(k).wait_send)


def run(far, rank, barred, qh, kvh):
    dma = pltpu.SemaphoreType.DMA
    bf16, f32 = jnp.bfloat16, jnp.float32
    return pl.pallas_call(
        functools.partial(kernel, far),
        out_shape=jax.ShapeDtypeStruct((PART, HEADS * HD), bf16),
        in_specs=[SMEM, SMEM, ANY, ANY],
        out_specs=VMEM,
        scratch_shapes=[
            pltpu.VMEM((SLOTS, 2, TILE, HD), bf16),
            pltpu.VMEM((SLOTS, 3, 3, 2, 2, TILE, HD), bf16),
            pltpu.VMEM((SLOTS, 2, 2, 2, TILE, HD), bf16),
            pltpu.VMEM((HD + 16, 2 * TILE), bf16),
            pltpu.VMEM((SLOTS, 2, 8, TILE), f32),
            pltpu.VMEM((SLOTS, 2, HD + 16, TILE), f32),
            pltpu.VMEM((SLOTS, 2, TILE, HD), bf16),
            pltpu.VMEM((HEADS, PART, HD), bf16),
            dma((SLOTS, CHIPS)),
            dma((CHIPS,)),
            dma((SLOTS,)),
            dma,
            dma((SLOTS, 5, 2)),
            dma((SLOTS, 5, 2)),
            dma((SLOTS,)),
            dma((SLOTS,)),
            dma((SLOTS,)),
            dma((SLOTS,)),
            dma((SLOTS, 2)),
            dma((SLOTS, 2)),
            dma((SLOTS,)),
            dma((SLOTS,)),
            dma((SLOTS, 8)),
            dma((SLOTS,)),
        ],
        compiler_params=pltpu.CompilerParams(collective_id=far, has_side_effects=True, vmem_limit_bytes=48 << 20),
        name=f"tile_attention{far}",
    )(rank, barred, qh, kvh)


def shards(queries, keys, values, windows):
    weight = windows[:, 1] * 4 + windows[:, 2] * 2 + windows[:, 0]
    index = jnp.arange(HEADS, dtype=jnp.int32)
    ahead = (weight[None, :] > weight[:, None]) | ((weight[None, :] == weight[:, None]) & (index[None, :] < index[:, None]))
    rank = jnp.sum(ahead.astype(jnp.int32), axis=1)
    found = rank[None, :] == index[:, None]
    perm = jnp.sum(jnp.where(found, index[None], 0), axis=1)
    barred = jnp.sum(jnp.where(found[:, :, None] & (windows[None] < 1), jnp.float32(1e30), 0.0), axis=1)
    far = (jnp.sum(windows[:, 1]) + CHIPS - 1) // CHIPS
    qh, kvh = pack(perm, queries, keys, values)
    return lax.switch(far, [functools.partial(run, n) for n in range(SLOTS + 1)], rank, barred, qh, kvh)


def solution(mesh):
    tokens = P(("slab", "head"), None)
    return jax.shard_map(
        shards, mesh=mesh, in_specs=(tokens, tokens, tokens, P()), out_specs=tokens, check_vma=False
    )
```

time: 1000 us -> 103 us (0.10)
  the two profiles are of different devices: /device:TPU:162 before, /device:TPU:7 now
where the time goes in v2:
time: 103 us; the launch traced here: 102 us
  Pallas kernels  97.7 us (95%)
  other arithmetic  2.46 us (2%)
    pallas_call x1, Pallas kernels, run(): pl.pallas_call(functools.partial(kernel, far), out_shape=jax.ShapeDtypeSt...  95.8 us

profile of v2, /device:TPU:7, one launch (start us, length us, event | category | flops | bytes accessed | tf_op | source)
XLA Modules:
  0.0 102.3 jit_solution(3311301937925354215)
XLA Ops:
  0.0 0.0 copy-start
  0.0 1.5 %add_bitcast_fusion = (s32[24]{0:T(128)S(1)}, s32[]{:T(128)}) fusion(s32[24,3]{0,1:T(4,128)} %param.11), kind=kLoop, calls=%fused_computation.14 | loop fusion | flops 119 | bytes 388 | tf_op jit(solution)/shard_map/add | solution.py:423
  2.1 0.2 convert_reduce_fusion
  2.3 0.7 select_reduce_fusion.4.perm
  3.0 1.9 %pack.1 = (bf16[24,96,128]{2,1,0:T(8,128)(2,1)S(1)}, bf16[24,2,96,128]{3,2,1,0:T(8,128)(2,1)S(1)}) custom-call(s32[24]{0:T(128)} %select_reduce_fusion.4.perm, bf16[96,3072]{1,0:T(8,128)(2,1)} %q_in.1, bf16[96,3072]{1,0:T(8,128)(2,1)} %k_in.1, bf16[96,3072]{1,0:T(8,128)(2,1)} %v_in.1), custom_call_target="tpu_custom_call" | custom-call | tf_op jit(solution)/shard_map/pack/pallas_call | solution.py:61
  4.9 0.0 copy-done
  4.9 96.5 %conditional.1 = (bf16[96,3072]{1,0:T(8,128)(2,1)S(1)}) conditional(s32[]{:T(128)} %clamp.3, (s32[24]{0:T(128)S(1)}, pred[24,24]{1,0:T(8,128)(4,1)S(1)}, bf16[24,96,128]{2,1,0:T(8,128)(2,1)S(1)}, bf16[24,2,96,128]{3,2,1,0:T(8,128)(2,1)S(1)}, f32[]{:T(128)}, /*index=5*/f32[]{:T(128)}, s32[24,3]{0,1:T(4,128)S(1)}, ...), branch_computations={%region_4.5_spmd.clone, %region_5.6_spmd.clone, %region_6.7_spmd.c... | conditional | flops 5184 | bytes 1892 | solution.py:432
  5.0 0.1 select_reduce_fusion.2
  5.1 0.1 copy.19.barred
  5.2 95.8 %tile_attention2.1 = bf16[96,3072]{1,0:T(8,128)(2,1)S(1)} custom-call(s32[24]{0:T(128)S(1)} %get-tuple-element.159.rank, f32[24,3]{1,0:T(8,128)S(1)} %copy.19.barred, bf16[3,8,96,128]{3,2,1,0:T(8,128)(2,1)S(1)} %bitcast.16, bf16[3,8,2,96,128]{4,3,2,1,0:T(8,128)(2,1)S(1)} %bitcast.12), custom_call_target="tpu_custom_call" | custom-call | tf_op jit(solution)/shard_map/cond/branch_2_fun/tile_attention2/pallas_call | solution.py:386
  101.5 0.8 copy.26
  (2 shorter events, 0.0 us)
Async XLA Ops:
  0.0 4.9 %copy-start = (s32[24,3]{0,1:T(4,128)S(1)}, s32[24,3]{0,1:T(4,128)}, u32[]{:S(2)}) copy-start(s32[24,3]{0,1:T(4,128)} %param.11) | copy-start | bytes 868

commit v3 on v2

--- a/solution.py
+++ b/solution.py
@@ -49,67 +49,89 @@
     ]
 
 
-def pack_kernel(perm, q_in, k_in, v_in, qh, kvh):
-    for r in range(HEADS):
-        cols = pl.ds(pl.multiple_of(perm[r] * HD, HD), HD)
+def pack_kernel(windows, q_in, k_in, v_in, qh, kvh, rank, barred, form):
+    key = [windows[e, 1] * 4 + windows[e, 2] * 2 + windows[e, 0] for e in range(HEADS)]
+    place = [jnp.int32(0)] * HEADS
+    for e in range(HEADS):
+        for f in range(e):
+            first = (key[f] >= key[e]).astype(jnp.int32)
+            place[e] += first
+            place[f] += 1 - first
+    tall = both = jnp.int32(0)
+    for e in range(HEADS):
+        r = place[e]
+        cols = pl.ds(e * HD, HD)
         qh[r] = q_in[:, cols]
         kvh[r, 0] = k_in[:, cols]
         kvh[r, 1] = v_in[:, cols]
-
-
-def pack(perm, queries, keys, values):
-    qh, kvh = pl.pallas_call(
+        rank[e] = r
+        tall += windows[e, 1]
+        both += windows[e, 1] * windows[e, 2]
+        for axis in range(3):
+            barred[r, axis] = jnp.where(windows[e, axis] > 0, 0.0, 1e30).astype(jnp.float32)
+    far = (tall + CHIPS - 1) // CHIPS
+    form[0] = jnp.where(far == 0, 0, 2 * far - 1 + (both > CHIPS * (far - 1)).astype(jnp.int32))
+
+
+def pack(windows, queries, keys, values):
+    qh, kvh, rank, barred, form = pl.pallas_call(
         pack_kernel,
         out_shape=(
             jax.ShapeDtypeStruct((HEADS, PART, HD), jnp.bfloat16),
             jax.ShapeDtypeStruct((HEADS, 2, PART, HD), jnp.bfloat16),
+            jax.ShapeDtypeStruct((HEADS,), jnp.int32),
+            jax.ShapeDtypeStruct((HEADS, 3), jnp.float32),
+            jax.ShapeDtypeStruct((1,), jnp.int32),
         ),
         in_specs=[SMEM, VMEM, VMEM, VMEM],
-        out_specs=(VMEM, VMEM),
+        out_specs=(VMEM, VMEM, SMEM, SMEM, SMEM),
         name="pack",
-    )(perm, queries, keys, values)
-    return qh.reshape(SLOTS, CHIPS, PART, HD), kvh.reshape(SLOTS, CHIPS, 2, PART, HD)
-
-
-def plan(far):
+    )(windows, queries, keys, values)
+    return form[0], rank, barred, qh.reshape(SLOTS, CHIPS, PART, HD), kvh.reshape(SLOTS, CHIPS, 2, PART, HD)
+
+
+def plan(far, wide):
     main = [("begin", 0)]
     for k in range(far):
         for hop in range(2, 6):
             for part in range(2):
-                main.append(("forward", k, hop, part))
-            if k == 0 and hop == 2:
+                main.append(("forward" if hop < 5 else "near", k, hop, part))
+            if k == 0 and hop == 3:
                 main.append(("begin", 1))
-            if k == 0 and hop == 5:
+            if (k, hop) == ((1, 3) if far == 3 else (far - 1, 4)):
                 main.append(("begin", 2))
-            if k > 0 and hop == 2:
+            if k > 0 and hop == 2 and k - 1 < wide:
                 main.append(("finish", k - 1))
             if k > 0 and hop == 4:
-                main.append(("share", k - 1))
+                main += [("share", k - 1, 0), ("share", k - 1, 1)]
     if far == 0:
         main += [("begin", 1), ("begin", 2)]
     else:
-        main += [("finish", far - 1), ("share", far - 1)]
+        main += [("finish", far - 1) if far <= wide else None, None, None, ("share", far - 1, 0), ("share", far - 1, 1)]
 
     def ready(event):
-        if event[0] == "begin":
-            k = event[1]
-            return [(0, k, "own"), (1, k, "inner")] + ([] if k < far else [(3, k, "outer")])
-        if event[0] == "forward":
-            k, hop, part = event[1:]
-            if part == 1 and hop == 2:
-                return [(0, k, "outer")]
-            if part == 1 and hop == 5:
-                return [(0, k, "near inner"), (1, k, "near own")]
-            return []
-        if event[0] == "finish":
-            return [(0, event[1], "near outer")]
-        return [(0, event[1], "side inner"), (1, event[1], "side own"), (4, event[1], "side outer")]
+        what, k = event[0], event[1]
+        if what == "begin" and k == 1:
+            return [(0, 0, "own"), (0, 0, "inner"), (0, 0, "outer"), (0, 1, "own"), (0, 1, "inner")] + (
+                [] if far > 1 else [(3, 1, "outer")]
+            )
+        if what == "begin" and k == 2:
+            return [(0, 2, "own"), (1, 2, "inner")] + ([] if far > 2 else [(3, 2, "outer")])
+        if what == "forward" and event[2:] == (2, 1) and k > 0:
+            return [(0, k, "outer")]
+        if what == "near" and event[3] == 1:
+            return [(0, k, "near inner"), (1, k, "near own")]
+        if what == "finish":
+            return [(0, k, "near outer")]
+        if what == "share" and event[2] == 1:
+            return [(0, k, "side inner"), (1, k, "side own")] + ([(3, k, "side outer")] if k < wide else [])
+        return []
 
     steps, pool = [], []
     n = 0
     while n < len(main) or pool:
         events = []
-        if n < len(main):
+        if n < len(main) and main[n]:
             events.append(main[n])
             pool += [(n + late, len(pool), k, what) for late, k, what in ready(main[n])]
         pool.sort(key=lambda p: p[0])
@@ -125,10 +147,10 @@
 
 
 def kernel(
-    far, rank, barred, qh, kvh, out,
+    far, wide, rank, barred, qh, kvh, out,
     q, kv, relay, vt, top, acc, o, back,
     a_send, q_send, kv_recv, q_recv, hop_send, hop_recv, own_send, own_recv,
-    mid_send, mid_recv, x_send, x_recv, xs_send, xs_recv, o_send, o_recv,
+    mid_send, mid_recv, x_send, x_recv, xs_send, xs_recv, halo_send, halo_recv, o_send, o_recv,
 ):
     x, y, z, c = coords()
     z_hi, x_lo, t = z // 4, x % 2, x // 2
@@ -150,33 +172,36 @@
     part = (y % 2) * 2 + c
     me = t * 4 + y
     rows = pl.ds(part * PART, PART)
-    copies = []
-
-    def send(src, dst, sem, recv, chip):
-        alone = (chip == me) & (c == y_hi)
-        to = device((chip // 4) * 2 + x_lo, chip % 4, z, y_hi)
-
-        @pl.when(alone)
-        def _():
-            pltpu.make_async_copy(src, dst, recv).start()
-
-        @pl.when(jnp.logical_not(alone))
-        def _():
-            remote(src, dst, sem, recv, to).start()
-
-        copies.append((alone, remote(src, dst, sem, recv, to)))
-
-    def scatter(k):
+    def spread(act):
+        def one(i, src, dst, sem, recv, chip):
+            copy = remote(src, dst, sem, recv, device((chip // 4) * 2 + x_lo, chip % 4, z, y_hi))
+            if i > 0:
+                act(copy)
+            else:
+                pl.when(c != y_hi)(lambda: act(copy))
+                if act is start:
+                    pl.when(c == y_hi)(pltpu.make_async_copy(src, dst, recv).start)
+
+        return one
+
+    def start(copy):
+        copy.start()
+
+    def sent(copy):
+        copy.wait_send()
+
+    def scatter(k, act):
+        for p in range(2):
+            for i in range(CHIPS):
+                chip = (me + i) % CHIPS
+                spread(act)(i, kvh.at[k, chip, p], kv.at[k, 1, 1, p, t, rows], a_send.at[k, p, i], kv_recv.at[k, p], chip)
+
+    def scatter_queries(act):
         for i in range(CHIPS):
             chip = (me + i) % CHIPS
-            send(kvh.at[k, chip], kv.at[k, 1, 1, :, t, rows], a_send.at[k, i], kv_recv.at[k], chip)
-
-    scatter(0)
-    for i in range(CHIPS):
-        chip = (me + i) % CHIPS
-        send(qh.at[:, chip], q.at[:, t, rows], q_send.at[i], q_recv, chip)
-    scatter(1)
-    scatter(2)
+            spread(act)(i, qh.at[:, chip], q.at[:, t, rows], q_send.at[i], q_recv, chip)
+
+    scatter(0, start)
     top[...] = jnp.full_like(top, -1e30)
     acc[...] = jnp.zeros_like(acc)
     vt[HD:] = jnp.ones((16, 2 * TILE), jnp.bfloat16)
@@ -189,6 +214,8 @@
     sender = x_lo == z_hi
     receiver = jnp.logical_not(sender)
     w_edge = jnp.where(c == 0, z % 4 > 0, z % 4 < 3)
+    halo_to = receiver & jnp.where(c == 0, z % 4 < 3, z % 4 > 0)
+    halo_from = receiver & w_edge
 
     def wait_for(place, sem):
         pltpu.make_async_copy(place, place, sem).wait()
@@ -223,12 +250,22 @@
     def mid_share(k):
         return remote(kv.at[k, near, inner], kv.at[k, near, 1], mid_send.at[k], mid_recv.at[k], twin)
 
-    def aside(k, n):
+    def aside(k, n, part):
         place = inner if n == 0 else outer
-        return remote(kv.at[k, near, place], kv.at[k, 2 - near, place], x_send.at[k, n], x_recv.at[k, n], side)
-
-    def side_share(k):
-        return remote(kv.at[k, 2 - near, inner], kv.at[k, 2 - near, 1], xs_send.at[k], xs_recv.at[k], twin)
+        return remote(
+            kv.at[k, near, place, part], kv.at[k, 2 - near, place, part], x_send.at[k, n, part], x_recv.at[k, n, part], side
+        )
+
+    def side_wait(k, n, part):
+        wait_for(kv.at[k, 2 - near, inner if n == 0 else outer, part], x_recv.at[k, n, part])
+
+    def side_share(k, part):
+        place = kv.at[k, 2 - near, inner, part]
+        return remote(place, kv.at[k, 2 - near, 1, part], xs_send.at[k, part], xs_recv.at[k, part], twin)
+
+    def halo(k, part):
+        place = kv.at[k, 2 - near, inner, part]
+        return remote(place, kv.at[k, 2 - near, outer, part], halo_send.at[part], halo_recv.at[part], ahead)
 
     def give_back(k, i):
         n = (t * 4 + part + i) % 8
@@ -240,29 +277,43 @@
     def communicate(event):
         what, k = event[0], event[1]
         if what == "begin":
-            wait_for(kv.at[k, 1, 1], kv_recv.at[k])
             for part in range(2):
+                wait_for(kv.at[k, 1, 1, part], kv_recv.at[k, part])
                 first_hop(k, part).start()
             own_share(k).start()
             if k == 0:
+                scatter_queries(start)
+                scatter(1, start)
+            if k == 1:
                 wait_for(q, q_recv)
+                scatter(2, start)
         elif what == "forward":
             hop, part = event[2:]
             hop_wait(k, hop - 1, part)
             next_hop(k, hop, part).start()
-            if hop == 5 and part == 1:
+        elif what == "near":
+            part = event[3]
+            hop_wait(k, 4, part)
+            if k < wide:
+                next_hop(k, 5, part).start()
+            pl.when(sender)(aside(k, 0, part).start)
+            if part == 1:
                 mid_share(k).start()
-                pl.when(sender)(aside(k, 0).start)
         elif what == "finish":
             for part in range(2):
                 hop_wait(k, 5, part)
-            pl.when(sender)(aside(k, 1).start)
+                if k < far - 1:
+                    pl.when(sender)(aside(k, 1, part).start)
         else:
+            part = event[2]
 
             @pl.when(receiver)
             def _():
-                wait_for(kv.at[k, 2 - near, inner], x_recv.at[k, 0])
-                side_share(k).start()
+                side_wait(k, 0, part)
+                side_share(k, part).start()
+
+            if k == far - 1 and k < wide:
+                pl.when(halo_to)(halo(k, part).start)
 
     def arrive(k, what):
         if what == "inner":
@@ -273,9 +324,21 @@
         elif what == "near own":
             wait_for(kv.at[k, near, 1], mid_recv.at[k])
         elif what == "side own":
-            pl.when(receiver)(lambda: wait_for(kv.at[k, 2 - near, 1], xs_recv.at[k]))
+
+            @pl.when(receiver)
+            def _():
+                for part in range(2):
+                    wait_for(kv.at[k, 2 - near, 1, part], xs_recv.at[k, part])
+
         elif what == "side outer":
-            pl.when(receiver)(lambda: wait_for(kv.at[k, 2 - near, outer], x_recv.at[k, 1]))
+
+            @pl.when(halo_from if k == far - 1 else receiver)
+            def _():
+                for part in range(2):
+                    if k == far - 1:
+                        wait_for(kv.at[k, 2 - near, outer, part], halo_recv.at[part])
+                    else:
+                        side_wait(k, 1, part)
 
     scale = HD ** (-0.5) * LOG2E
 
@@ -323,7 +386,7 @@
             else:
                 copy.start()
 
-    steps = plan(far)
+    steps = plan(far, wide)
     last = {}
     for n, (events, pick) in enumerate(steps):
         if pick:
@@ -343,7 +406,7 @@
             if pick:
                 code = jnp.where(n == m, pick[0] * 9 + PLACES.index(pick[1]), code)
 
-        @pl.when((code >= 0) & ((code % 9 < 6) | receiver))
+        @pl.when((code >= 0) & ((code % 9 < 6) | receiver) & ((code % 9 != 8) | halo_from))
         def _():
             attention(code // 9, code % 9)
 
@@ -358,9 +421,9 @@
     for e in range(HEADS):
         out[:, e * HD : (e + 1) * HD] = back[rank[e]]
 
-    for alone, copy in copies:
-        pl.when(jnp.logical_not(alone))(copy.wait_send)
+    scatter_queries(sent)
     for k in range(SLOTS):
+        scatter(k, sent)
         for part_ in range(2):
             first_hop(k, part_).wait_send()
         own_share(k).wait_send()
@@ -371,20 +434,23 @@
             else:
                 copy.wait_send()
     for k in range(far):
-        for hop in range(2, 6):
+        for hop in range(2, 6 if k < wide else 5):
             for part_ in range(2):
                 next_hop(k, hop, part_).wait_send()
         mid_share(k).wait_send()
-        for n in range(2):
-            pl.when(sender)(aside(k, n).wait_send)
-        pl.when(receiver)(side_share(k).wait_send)
-
-
-def run(far, rank, barred, qh, kvh):
+        for part_ in range(2):
+            for n in range(2 if k < min(wide, far - 1) else 1):
+                pl.when(sender)(aside(k, n, part_).wait_send)
+            pl.when(receiver)(side_share(k, part_).wait_send)
+            if k == far - 1 and k < wide:
+                pl.when(halo_to)(halo(k, part_).wait_send)
+
+
+def run(far, wide, rank, barred, qh, kvh):
     dma = pltpu.SemaphoreType.DMA
     bf16, f32 = jnp.bfloat16, jnp.float32
     return pl.pallas_call(
-        functools.partial(kernel, far),
+        functools.partial(kernel, far, wide),
         out_shape=jax.ShapeDtypeStruct((PART, HEADS * HD), bf16),
         in_specs=[SMEM, SMEM, ANY, ANY],
         out_specs=VMEM,
@@ -397,9 +463,9 @@
             pltpu.VMEM((SLOTS, 2, HD + 16, TILE), f32),
             pltpu.VMEM((SLOTS, 2, TILE, HD), bf16),
             pltpu.VMEM((HEADS, PART, HD), bf16),
-            dma((SLOTS, CHIPS)),
+            dma((SLOTS, 2, CHIPS)),
             dma((CHIPS,)),
-            dma((SLOTS,)),
+            dma((SLOTS, 2)),
             dma,
             dma((SLOTS, 5, 2)),
             dma((SLOTS, 5, 2)),
@@ -407,29 +473,24 @@
             dma((SLOTS,)),
             dma((SLOTS,)),
             dma((SLOTS,)),
+            dma((SLOTS, 2, 2)),
+            dma((SLOTS, 2, 2)),
             dma((SLOTS, 2)),
             dma((SLOTS, 2)),
-            dma((SLOTS,)),
-            dma((SLOTS,)),
+            dma((2,)),
+            dma((2,)),
             dma((SLOTS, 8)),
             dma((SLOTS,)),
         ],
-        compiler_params=pltpu.CompilerParams(collective_id=far, has_side_effects=True, vmem_limit_bytes=48 << 20),
-        name=f"tile_attention{far}",
+        compiler_params=pltpu.CompilerParams(collective_id=far * 4 + wide, has_side_effects=True, vmem_limit_bytes=48 << 20),
+        name=f"tile_attention{far}{wide}",
     )(rank, barred, qh, kvh)
 
 
 def shards(queries, keys, values, windows):
-    weight = windows[:, 1] * 4 + windows[:, 2] * 2 + windows[:, 0]
-    index = jnp.arange(HEADS, dtype=jnp.int32)
-    ahead = (weight[None, :] > weight[:, None]) | ((weight[None, :] == weight[:, None]) & (index[None, :] < index[:, None]))
-    rank = jnp.sum(ahead.astype(jnp.int32), axis=1)
-    found = rank[None, :] == index[:, None]
-    perm = jnp.sum(jnp.where(found, index[None], 0), axis=1)
-    barred = jnp.sum(jnp.where(found[:, :, None] & (windows[None] < 1), jnp.float32(1e30), 0.0), axis=1)
-    far = (jnp.sum(windows[:, 1]) + CHIPS - 1) // CHIPS
-    qh, kvh = pack(perm, queries, keys, values)
-    return lax.switch(far, [functools.partial(run, n) for n in range(SLOTS + 1)], rank, barred, qh, kvh)
+    form, rank, barred, qh, kvh = pack(windows, queries, keys, values)
+    forms = [(0, 0), (1, 0), (1, 1), (2, 1), (2, 2), (3, 2), (3, 3)]
+    return lax.switch(form, [functools.partial(run, *f) for f in forms], rank, barred, qh, kvh)
 
 
 def solution(mesh):

time: 103 us -> 90.7 us (0.88)
  Pallas kernels: 97.7 us -> 86.5 us
  other arithmetic: 2.46 us -> 0 us
  local copies, waits for them, and re-layouts: 0.91 us -> 2.18 us
    pallas_call x1, Pallas kernels: 95.8 us -> 83.1 us  [run(): pl.pallas_call(functools.partial(kernel, far, wide), out_shape=jax.ShapeD...]
    pallas_call x1, Pallas kernels: 1.89 us -> 3.35 us  [pack(): pl.pallas_call(pack_kernel, out_shape=(jax.ShapeDtypeStruct((HEADS, PART,...]
    add x1 -> x0, other arithmetic: 1.46 us -> none  [shards(): weight = windows[:, 1] * 4 + windows[:, 2] * 2 + windows[:, 0]]
    unnamed x3 -> x2, local copies, waits for them, and re-layouts: 0.82 us -> 2.18 us
where the time goes in v3:
time: 90.7 us; the launch traced here: 89.9 us
  Pallas kernels  86.5 us (95%)
  local copies, waits for them, and re-layouts  2.18 us (2%)
    pallas_call x1, Pallas kernels, run(): pl.pallas_call(functools.partial(kernel, far, wide), out_shape=jax.ShapeD...  83.1 us
    pallas_call x1, Pallas kernels, pack(): pl.pallas_call(pack_kernel, out_shape=(jax.ShapeDtypeStruct((HEADS, PART,...  3.35 us
    unnamed x2, local copies, waits for them, and re-layouts  2.18 us

profile of v3, /device:TPU:7, one launch (start us, length us, event | category | flops | bytes accessed | tf_op | source)
XLA Modules:
  0.0 89.9 jit_solution(16067017716291068148)
XLA Ops:
  0.0 1.4 %copy.12.windows = s32[24,3]{1,0:T(8,128)} copy(s32[24,3]{0,1:T(4,128)} %param.14) | data formatting | bytes 576 | tf_op args[3]
  1.4 3.4 %pack.1 = (bf16[24,96,128]{2,1,0:T(8,128)(2,1)S(1)}, bf16[24,2,96,128]{3,2,1,0:T(8,128)(2,1)S(1)}, s32[24]{0:T(128)S(1)}, f32[24,3]{1,0:T(8,128)S(1)}, s32[1]{0:T(128)}) custom-call(s32[24,3]{1,0:T(8,128)} %copy.12.windows, bf16[96,3072]{1,0:T(8,128)(2,1)} %q_in.1, bf16[96,3072]{1,0:T(8,128)(2,1)} %k_in.1, bf16[96,3072]{1,0:T(8,128)(2,1)} %v_in.1), custom_call_target="tpu_custom_call" | custom-call | tf_op jit(solution)/shard_map/pack/pallas_call | solution.py:77
  5.4 83.7 %conditional.1 = (bf16[96,3072]{1,0:T(8,128)(2,1)S(1)}) conditional(s32[]{:T(128)} %bitcast, (s32[24]{0:T(128)S(1)}, f32[24,3]{1,0:T(8,128)S(1)}, bf16[3,8,96,128]{3,2,1,0:T(8,128)(2,1)S(1)}, bf16[3,8,2,96,128]{4,3,2,1,0:T(8,128)(2,1)S(1)}) %tuple.48, (s32[24]{0:T(128)S(1)}, f32[24,3]{1,0:T(8,128)S(1)}, ...), branch_computations={%region_0.0_spmd, %region_1.0_spmd, %region_2.0_spmd, %region_3.0_... | conditional | bytes 8 | solution.py:493
  5.7 83.1 %tile_attention21.1 = bf16[96,3072]{1,0:T(8,128)(2,1)S(1)} custom-call(s32[24]{0:T(128)S(1)} %get-tuple-element.81.rank, f32[24,3]{1,0:T(8,128)S(1)} %get-tuple-element.82.barred, bf16[3,8,96,128]{3,2,1,0:T(8,128)(2,1)S(1)} %get-tuple-element.83.qh, bf16[3,8,2,96,128]{4,3,2,1,0:T(8,128)(2,1)S(1)} %get-tuple-element.84.kvh), custom_call_target="tpu_custom_call" | custom-call | tf_op jit(solution)/shard_map/cond/branch_3_fun/tile_attention21/pallas_call | solution.py:452
  89.1 0.8 copy.21

commit v4 on v3

--- a/solution.py
+++ b/solution.py
@@ -49,7 +49,13 @@
     ]
 
 
-def pack_kernel(windows, q_in, k_in, v_in, qh, kvh, rank, barred, form):
+def pack_kernel(windows, q_hbm, k_hbm, v_hbm, qh, kvh, rank, barred, form, q_in, k_in, v_in, sem):
+    loads = [
+        pltpu.make_async_copy(src, dst, sem.at[i])
+        for i, (src, dst) in enumerate([(k_hbm, k_in), (v_hbm, v_in), (q_hbm, q_in)])
+    ]
+    for load in loads:
+        load.start()
     key = [windows[e, 1] * 4 + windows[e, 2] * 2 + windows[e, 0] for e in range(HEADS)]
     place = [jnp.int32(0)] * HEADS
     for e in range(HEADS):
@@ -60,10 +66,6 @@
     tall = both = jnp.int32(0)
     for e in range(HEADS):
         r = place[e]
-        cols = pl.ds(e * HD, HD)
-        qh[r] = q_in[:, cols]
-        kvh[r, 0] = k_in[:, cols]
-        kvh[r, 1] = v_in[:, cols]
         rank[e] = r
         tall += windows[e, 1]
         both += windows[e, 1] * windows[e, 2]
@@ -71,6 +73,14 @@
             barred[r, axis] = jnp.where(windows[e, axis] > 0, 0.0, 1e30).astype(jnp.float32)
     far = (tall + CHIPS - 1) // CHIPS
     form[0] = jnp.where(far == 0, 0, 2 * far - 1 + (both > CHIPS * (far - 1)).astype(jnp.int32))
+    for load in loads:
+        load.wait()
+    for e in range(HEADS):
+        r = place[e]
+        cols = pl.ds(e * HD, HD)
+        qh[r] = q_in[:, cols]
+        kvh[r, 0] = k_in[:, cols]
+        kvh[r, 1] = v_in[:, cols]
 
 
 def pack(windows, queries, keys, values):
@@ -83,35 +93,40 @@
             jax.ShapeDtypeStruct((HEADS, 3), jnp.float32),
             jax.ShapeDtypeStruct((1,), jnp.int32),
         ),
-        in_specs=[SMEM, VMEM, VMEM, VMEM],
+        in_specs=[SMEM, ANY, ANY, ANY],
         out_specs=(VMEM, VMEM, SMEM, SMEM, SMEM),
+        scratch_shapes=[pltpu.VMEM((PART, HEADS * HD), jnp.bfloat16)] * 3 + [pltpu.SemaphoreType.DMA((3,))],
         name="pack",
     )(windows, queries, keys, values)
     return form[0], rank, barred, qh.reshape(SLOTS, CHIPS, PART, HD), kvh.reshape(SLOTS, CHIPS, 2, PART, HD)
 
 
 def plan(far, wide):
-    main = [("begin", 0)]
-    for k in range(far):
-        for hop in range(2, 6):
-            for part in range(2):
-                main.append(("forward" if hop < 5 else "near", k, hop, part))
-            if k == 0 and hop == 3:
-                main.append(("begin", 1))
-            if (k, hop) == ((1, 3) if far == 3 else (far - 1, 4)):
+    def hops(k, hop):
+        return [("forward" if hop < 5 else "near", k, hop, part) for part in range(2)]
+
+    if far == 0:
+        main = [("begin", 0), ("ask", 0), ("begin", 1), ("queries", 0), ("begin", 2)]
+    else:
+        main = [("begin", 0)] + hops(0, 2) + [("ask", 0)] + hops(0, 3) + [("begin", 1)] + hops(0, 4) + [("queries", 0)]
+        if far == 1:
+            main.append(("begin", 2))
+        for k in range(1, far):
+            main += hops(k, 2) + hops(k - 1, 5) + hops(k, 3)
+            if (far, k) == (3, 1):
                 main.append(("begin", 2))
-            if k > 0 and hop == 2 and k - 1 < wide:
+            if k - 1 < wide:
                 main.append(("finish", k - 1))
-            if k > 0 and hop == 4:
-                main += [("share", k - 1, 0), ("share", k - 1, 1)]
-    if far == 0:
-        main += [("begin", 1), ("begin", 2)]
-    else:
-        main += [("finish", far - 1) if far <= wide else None, None, None, ("share", far - 1, 0), ("share", far - 1, 1)]
+            main += hops(k, 4)
+            if far == 2:
+                main.append(("begin", 2))
+            main += [("share", k - 1, 0), ("share", k - 1, 1)]
+        main += hops(far - 1, 5) + [("finish", far - 1) if far <= wide else None, None, None]
+        main += [("share", far - 1, 0), ("share", far - 1, 1)]
 
     def ready(event):
         what, k = event[0], event[1]
-        if what == "begin" and k == 1:
+        if what == "queries":
             return [(0, 0, "own"), (0, 0, "inner"), (0, 0, "outer"), (0, 1, "own"), (0, 1, "inner")] + (
                 [] if far > 1 else [(3, 1, "outer")]
             )
@@ -281,12 +296,12 @@
                 wait_for(kv.at[k, 1, 1, part], kv_recv.at[k, part])
                 first_hop(k, part).start()
             own_share(k).start()
-            if k == 0:
-                scatter_queries(start)
-                scatter(1, start)
-            if k == 1:
-                wait_for(q, q_recv)
-                scatter(2, start)
+            if k < 2:
+                scatter(k + 1, start)
+        elif what == "ask":
+            scatter_queries(start)
+        elif what == "queries":
+            wait_for(q, q_recv)
         elif what == "forward":
             hop, part = event[2:]
             hop_wait(k, hop - 1, part)

time: 90.7 us -> 88.8 us (0.979)
  Pallas kernels: 86.5 us -> 85.2 us
    pallas_call x1, Pallas kernels: 83.1 us -> 81.8 us  [run(): pl.pallas_call(functools.partial(kernel, far, wide), out_shape=jax.ShapeD...]
where the time goes in v4:
time: 88.8 us; the launch traced here: 88.6 us
  Pallas kernels  85.2 us (96%)
  local copies, waits for them, and re-layouts  2.18 us (2%)
    pallas_call x1, Pallas kernels, run(): pl.pallas_call(functools.partial(kernel, far, wide), out_shape=jax.ShapeD...  81.8 us
    pallas_call x1, Pallas kernels, pack(): pl.pallas_call(pack_kernel, out_shape=(jax.ShapeDtypeStruct((HEADS, PART,...  3.41 us
    unnamed x2, local copies, waits for them, and re-layouts  2.18 us

profile of v4, /device:TPU:7, one launch (start us, length us, event | category | flops | bytes accessed | tf_op | source)
XLA Modules:
  0.0 88.6 jit_solution(17306065860265013598)
XLA Ops:
  0.0 1.4 %copy.12.windows = s32[24,3]{1,0:T(8,128)} copy(s32[24,3]{0,1:T(4,128)} %param.14) | data formatting | bytes 576 | tf_op args[3]
  1.4 3.4 %pack.1 = (bf16[24,96,128]{2,1,0:T(8,128)(2,1)S(1)}, bf16[24,2,96,128]{3,2,1,0:T(8,128)(2,1)S(1)}, s32[24]{0:T(128)S(1)}, f32[24,3]{1,0:T(8,128)S(1)}, s32[1]{0:T(128)}) custom-call(s32[24,3]{1,0:T(8,128)} %copy.12.windows, bf16[96,3072]{1,0:T(8,128)(2,1)} %q_hbm.1, bf16[96,3072]{1,0:T(8,128)(2,1)} %k_hbm.1, bf16[96,3072]{1,0:T(8,128)(2,1)} %v_hbm.1), custom_call_target="tpu_custom_call" | custom-call | tf_op jit(solution)/shard_map/pack/pallas_call | solution.py:87
  5.5 82.3 %conditional.1 = (bf16[96,3072]{1,0:T(8,128)(2,1)S(1)}) conditional(s32[]{:T(128)} %bitcast, (s32[24]{0:T(128)S(1)}, f32[24,3]{1,0:T(8,128)S(1)}, bf16[3,8,96,128]{3,2,1,0:T(8,128)(2,1)S(1)}, bf16[3,8,2,96,128]{4,3,2,1,0:T(8,128)(2,1)S(1)}) %tuple.48, (s32[24]{0:T(128)S(1)}, f32[24,3]{1,0:T(8,128)S(1)}, ...), branch_computations={%region_0.0_spmd, %region_1.0_spmd, %region_2.0_spmd, %region_3.0_... | conditional | bytes 8 | solution.py:508
  5.7 81.8 %tile_attention21.1 = bf16[96,3072]{1,0:T(8,128)(2,1)S(1)} custom-call(s32[24]{0:T(128)S(1)} %get-tuple-element.81.rank, f32[24,3]{1,0:T(8,128)S(1)} %get-tuple-element.82.barred, bf16[3,8,96,128]{3,2,1,0:T(8,128)(2,1)S(1)} %get-tuple-element.83.qh, bf16[3,8,2,96,128]{4,3,2,1,0:T(8,128)(2,1)S(1)} %get-tuple-element.84.kvh), custom_call_target="tpu_custom_call" | custom-call | tf_op jit(solution)/shard_map/cond/branch_3_fun/tile_attention21/pallas_call | solution.py:467
  87.8 0.8 copy.21

commit v5 on v4

--- a/solution.py
+++ b/solution.py
@@ -49,28 +49,39 @@
     ]
 
 
-def pack_kernel(windows, q_hbm, k_hbm, v_hbm, qh, kvh, rank, barred, form, q_in, k_in, v_in, sem):
+def pack_kernel(reach, q_hbm, k_hbm, v_hbm, qh, kvh, rank, barred, form, windows, count, q_in, k_in, v_in, sem):
+    look = pltpu.make_async_copy(reach, windows, sem.at[3])
+    look.start()
     loads = [
         pltpu.make_async_copy(src, dst, sem.at[i])
         for i, (src, dst) in enumerate([(k_hbm, k_in), (v_hbm, v_in), (q_hbm, q_in)])
     ]
     for load in loads:
         load.start()
-    key = [windows[e, 1] * 4 + windows[e, 2] * 2 + windows[e, 0] for e in range(HEADS)]
-    place = [jnp.int32(0)] * HEADS
+    for b in range(8):
+        count[b] = 0
+    look.wait()
+    key = [windows[1, e] * 4 + windows[2, e] * 2 + windows[0, e] for e in range(HEADS)]
     for e in range(HEADS):
-        for f in range(e):
-            first = (key[f] >= key[e]).astype(jnp.int32)
-            place[e] += first
-            place[f] += 1 - first
+        count[key[e]] = count[key[e]] + 1
+    ahead = jnp.int32(0)
+    for b in reversed(range(8)):
+        here = count[b]
+        count[b] = ahead
+        ahead += here
+    place = []
+    for e in range(HEADS):
+        r = count[key[e]]
+        count[key[e]] = r + 1
+        place.append(r)
     tall = both = jnp.int32(0)
     for e in range(HEADS):
         r = place[e]
         rank[e] = r
-        tall += windows[e, 1]
-        both += windows[e, 1] * windows[e, 2]
+        tall += windows[1, e]
+        both += windows[1, e] * windows[2, e]
         for axis in range(3):
-            barred[r, axis] = jnp.where(windows[e, axis] > 0, 0.0, 1e30).astype(jnp.float32)
+            barred[r, axis] = jnp.where(windows[axis, e] > 0, 0.0, 1e30).astype(jnp.float32)
     far = (tall + CHIPS - 1) // CHIPS
     form[0] = jnp.where(far == 0, 0, 2 * far - 1 + (both > CHIPS * (far - 1)).astype(jnp.int32))
     for load in loads:
@@ -93,11 +104,13 @@
             jax.ShapeDtypeStruct((HEADS, 3), jnp.float32),
             jax.ShapeDtypeStruct((1,), jnp.int32),
         ),
-        in_specs=[SMEM, ANY, ANY, ANY],
+        in_specs=[ANY, ANY, ANY, ANY],
         out_specs=(VMEM, VMEM, SMEM, SMEM, SMEM),
-        scratch_shapes=[pltpu.VMEM((PART, HEADS * HD), jnp.bfloat16)] * 3 + [pltpu.SemaphoreType.DMA((3,))],
+        scratch_shapes=[pltpu.SMEM((3, HEADS), jnp.int32), pltpu.SMEM((8,), jnp.int32)]
+        + [pltpu.VMEM((PART, HEADS * HD), jnp.bfloat16)] * 3
+        + [pltpu.SemaphoreType.DMA((4,))],
         name="pack",
-    )(windows, queries, keys, values)
+    )(windows.T, queries, keys, values)
     return form[0], rank, barred, qh.reshape(SLOTS, CHIPS, PART, HD), kvh.reshape(SLOTS, CHIPS, 2, PART, HD)
 
 

time: 88.8 us -> 86.5 us (0.974)
  local copies, waits for them, and re-layouts: 2.18 us -> 0.82 us
  Pallas kernels: 85.2 us -> 84.3 us
    unnamed x2 -> x1, local copies, waits for them, and re-layouts: 2.18 us -> 0.82 us
where the time goes in v5:
time: 86.5 us; the launch traced here: 86.4 us
  Pallas kernels  84.3 us (97%)
    pallas_call x1, Pallas kernels, run(): pl.pallas_call(functools.partial(kernel, far, wide), out_shape=jax.ShapeD...  81.7 us
    pallas_call x1, Pallas kernels, pack(): pl.pallas_call(pack_kernel, out_shape=(jax.ShapeDtypeStruct((HEADS, PART,...  2.56 us

profile of v5, /device:TPU:7, one launch (start us, length us, event | category | flops | bytes accessed | tf_op | source)
XLA Modules:
  0.0 86.4 jit_solution(16033806444308951821)
XLA Ops:
  0.0 2.6 %pack.1 = (bf16[24,96,128]{2,1,0:T(8,128)(2,1)S(1)}, bf16[24,2,96,128]{3,2,1,0:T(8,128)(2,1)S(1)}, s32[24]{0:T(128)S(1)}, f32[24,3]{1,0:T(8,128)S(1)}, s32[1]{0:T(128)}) custom-call(s32[3,24]{1,0:T(4,128)} %bitcast.18, bf16[96,3072]{1,0:T(8,128)(2,1)} %q_hbm.1, bf16[96,3072]{1,0:T(8,128)(2,1)} %k_hbm.1, bf16[96,3072]{1,0:T(8,128)(2,1)} %v_hbm.1), custom_call_target="tpu_custom_call" | custom-call | tf_op jit(solution)/shard_map/pack/pallas_call | solution.py:98
  3.2 82.3 %conditional.1 = (bf16[96,3072]{1,0:T(8,128)(2,1)S(1)}) conditional(s32[]{:T(128)} %bitcast.1, (s32[24]{0:T(128)S(1)}, f32[24,3]{1,0:T(8,128)S(1)}, bf16[3,8,96,128]{3,2,1,0:T(8,128)(2,1)S(1)}, bf16[3,8,2,96,128]{4,3,2,1,0:T(8,128)(2,1)S(1)}) %tuple.48, (s32[24]{0:T(128)S(1)}, f32[24,3]{1,0:T(8,128)S(1)}, ...), branch_computations={%region_0.0_spmd, %region_1.0_spmd, %region_2.0_spmd, %region_3.0_... | conditional | bytes 8 | solution.py:521
  3.5 81.7 %tile_attention21.1 = bf16[96,3072]{1,0:T(8,128)(2,1)S(1)} custom-call(s32[24]{0:T(128)S(1)} %get-tuple-element.81.rank, f32[24,3]{1,0:T(8,128)S(1)} %get-tuple-element.82.barred, bf16[3,8,96,128]{3,2,1,0:T(8,128)(2,1)S(1)} %get-tuple-element.83.qh, bf16[3,8,2,96,128]{4,3,2,1,0:T(8,128)(2,1)S(1)} %get-tuple-element.84.kvh), custom_call_target="tpu_custom_call" | custom-call | tf_op jit(solution)/shard_map/cond/branch_3_fun/tile_attention21/pallas_call | solution.py:480
  85.5 0.8 copy.20
